TPU v7x, 32 devices: a whole 2x2x4 slice. The times are simulated.
32 devices in a mesh: stream: 4 (over y, x), tm: 8 (over z, core).
Axes of the slice: x: 2, y: 2, z: 4, core: 2. Of those that a mesh axis runs over, the one named last changes fastest.
Arguments:
- frames: bfloat16 [16, 8, 256, 512], P('stream', 'tm'), may hold values from -6 to 6
- space_gain: float32 [512], replicated, may hold values from 0.1 to 1.9
- space_input: bfloat16 [512, 1536], replicated, may hold values from -0.25 to 0.25
- space_output: bfloat16 [512, 512], replicated, may hold values from -2 to 2
- space_scale: float32 [512], replicated, may hold values from 0.1 to 1.9
- space_up: bfloat16 [512, 2048], replicated, may hold values from -0.25 to 0.25
- space_down: bfloat16 [2048, 512], replicated, may hold values from -0.125 to 0.125
- time_gain: float32 [512], replicated, may hold values from 0.1 to 1.9
- time_input: bfloat16 [512, 1536], replicated, may hold values from -0.25 to 0.25
- time_output: bfloat16 [512, 512], replicated, may hold values from -1 to 1
- time_scale: float32 [512], replicated, may hold values from 0.1 to 1.9
- time_up: bfloat16 [512, 2048], replicated, may hold values from -0.25 to 0.25
- time_down: bfloat16 [2048, 512], replicated, may hold values from -0.125 to 0.125
- clip_labels: int32 [16, 8], P('stream'), may hold values from 0 to 7, as said below
- output_grad: bfloat16 [16, 8, 256, 512], P('stream', 'tm'), may hold values from -6 to 6
Outputs:
- block_out: float32 [16, 8, 256, 512], P('stream', 'tm')
- input_grad: float32 [16, 8, 256, 512], P('stream', 'tm')
- space_gain_grad: float32 [512], P('tm')
- space_input_grad: float32 [512, 1536], P('tm')
- space_output_grad: float32 [512, 512], P('tm')
- space_scale_grad: float32 [512], P('tm')
- space_up_grad: float32 [512, 2048], P('tm')
- space_down_grad: float32 [2048, 512], P('tm')
- time_gain_grad: float32 [512], P('tm')
- time_input_grad: float32 [512, 1536], P('tm')
- time_output_grad: float32 [512, 512], P('tm')
- time_scale_grad: float32 [512], P('tm')
- time_up_grad: float32 [512, 2048], P('tm')
- time_down_grad: float32 [2048, 512], P('tm')
Inputs may be any that keep to these rules, and one draw needn't show every extreme that they name: `clip_labels`: in every pack the labels start at 0 and rise by 0 or 1 from one frame-slot to the next; frame-slots with one label form a clip. In each aligned group of 4 packs one pack is a single clip over all 8 frame-slots, and another pack has a clip of one frame-slot at every frame-slot.
All inputs are finite; a program needn't handle non-finite values.
Results may differ from a plain program's by a relative error of at most 0.025.
Values may be sent and summed in bfloat16 or wider, within the bound.
No kernel may reach another device: no remote copies, remote signals or barrier semaphores. Data moves between devices by JAX's collectives and lax.ppermute only.
A program may use at most 192 MiB of HBM per device.

v0:
```python
import functools

import jax
import jax.numpy as jnp
from jax import lax
from jax.experimental import pallas as pl
from jax.experimental.pallas import tpu as pltpu
from jax.sharding import PartitionSpec as P

HEADS = 8
EPS = 1e-05
GELU_A = 0.7978845608028654
GELU_B = 0.044715
BF = jnp.bfloat16
F32 = jnp.float32
CHUNK = 512
LANES = 128
COST = 1
ROWS = (0, 96, 64, 80, 160, 176)
VMEM = 60 * 1024 * 1024
SMALL_VMEM = 24 * 1024 * 1024


def nn(a, b):
    return jnp.dot(a, b, preferred_element_type=F32)


def nt(a, b):
    return lax.dot_general(a, b, (((1,), (1,)), ((), ())), preferred_element_type=F32)


def tn(a, b):
    return lax.dot_general(a, b, (((0,), (0,)), ((), ())), preferred_element_type=F32)


def unit(values):
    average = jnp.mean(values, axis=-1, keepdims=True)
    centered = values - average
    inverse = lax.rsqrt(jnp.mean(centered * centered, axis=-1, keepdims=True) + EPS)
    return centered * inverse, inverse


def unit_backward(grad, unit_rows, inverse):
    first = jnp.mean(grad, axis=-1, keepdims=True)
    second = jnp.mean(grad * unit_rows, axis=-1, keepdims=True)
    return inverse * (grad - first - unit_rows * second)


def gelu_parts(u):
    square = u * u
    tangent = jnp.tanh(u * (BF(GELU_A) + BF(GELU_A * GELU_B) * square))
    half = BF(0.5) * u
    value = half + half * tangent
    slope = (BF(0.5) + BF(0.5) * tangent) + half * (BF(1.0) - tangent * tangent) * (
        BF(GELU_A) + BF(3.0 * GELU_A * GELU_B) * square
    )
    return value, slope


def head_masks(width):
    lane = lax.broadcasted_iota(jnp.int32, (1, 2 * width), 1)
    low = lane < width
    return low, (low.astype(F32).astype(BF), (1.0 - low.astype(F32)).astype(BF))


def attend_steps(qkv_ref, p_ref, o_ref, bias_ref, s_ref):
    width = qkv_ref.shape[1] // 3
    size = width // HEADS
    _, masks = head_masks(size)

    def lanes(part, head):
        at = part * width + (head // 2) * 2 * size
        return qkv_ref[:, at : at + 2 * size]

    def score(head):
        s_ref[head % 4] = nt(lanes(1, head) * masks[head % 2], lanes(0, head) * BF(size**-0.5))

    def soften(head):
        scores = s_ref[head % 4]
        if bias_ref is not None:
            scores = scores + bias_ref[...]
        e = jnp.exp(scores - jnp.max(scores, axis=0, keepdims=True))
        p_ref[head] = (e * (1.0 / jnp.sum(e, axis=0, keepdims=True))).astype(BF)

    for head in range(0, HEADS, 2):
        if head == 0:
            score(0)
            score(1)
        if head + 2 < HEADS:
            score(head + 2)
            score(head + 3)
        soften(head)
        soften(head + 1)
        yield
    for head in range(0, HEADS, 2):
        v = lanes(2, head).T
        both = jnp.concatenate([nn(v[:size], p_ref[head]), nn(v[size:], p_ref[head + 1])], axis=0)
        o_ref[:, head * size : (head + 2) * size] = both.T.astype(BF)
        yield


def attend_backward_steps(qkv_ref, p_ref, go_ref, out_ref, gp_ref, gs_ref):
    width = qkv_ref.shape[1] // 3
    size = width // HEADS
    _, masks = head_masks(size)

    def lanes(part, head):
        at = part * width + (head // 2) * 2 * size
        return qkv_ref[:, at : at + 2 * size]

    def gos(head):
        return go_ref[:, (head // 2) * 2 * size : (head // 2 + 1) * 2 * size]

    def put(part, head, value):
        at = part * width + head * size
        out_ref[:, at : at + 2 * size] = value.astype(BF)

    def start(head):
        for h in (head, head + 1):
            gp_ref[h % 4] = nt(lanes(2, h) * masks[h % 2], gos(h)).astype(BF)
        g = gos(head)
        put(2, head, nn(p_ref[head], g * masks[0]) + nn(p_ref[head + 1], g * masks[1]))

    def middle(head):
        p = p_ref[head]
        weighted = p * gp_ref[head % 4]
        total = jnp.sum(weighted.astype(F32), axis=0, keepdims=True).astype(BF)
        gs_ref[head] = weighted - p * total

    def finish(head):
        q = lanes(0, head) * BF(size**-0.5)
        k = (lanes(1, head) * BF(size**-0.5)).T
        put(1, head, nn(gs_ref[head], q * masks[0]) + nn(gs_ref[head + 1], q * masks[1]))
        both = jnp.concatenate([nn(k[:size], gs_ref[head]), nn(k[size:], gs_ref[head + 1])], axis=0)
        put(0, head, both.T)

    start(0)
    yield
    for head in range(0, HEADS, 2):
        middle(head)
        middle(head + 1)
        if head + 2 < HEADS:
            start(head + 2)
        if head > 0:
            finish(head - 2)
        yield
    finish(HEADS - 2)


def feed_up_steps(m, up_ref, down_ref, h_ref, slope_ref, u_ref):
    steps = up_ref.shape[1] // CHUNK

    def before(step):
        u_ref[step % 2] = nn(m, up_ref[:, step * CHUNK : (step + 1) * CHUNK]).astype(BF)

    before(0)
    for step in range(steps):
        if step + 1 < steps:
            before(step + 1)
        at = step * CHUNK
        h_ref[:, at : at + CHUNK], slope_ref[:, at : at + CHUNK] = gelu_parts(u_ref[step % 2])
        yield
    return nn(h_ref[...], down_ref[...])


def feed_back_steps(e2, up_ref, down_ref, slope_ref, eu_ref, up_copy=None):
    for at in range(0, up_ref.shape[1], CHUNK):
        gh = nt(e2, down_ref[at : at + CHUNK, :]).astype(BF)
        eu_ref[:, at : at + CHUNK] = gh * slope_ref[:, at : at + CHUNK]
        yield
    if up_copy is not None:
        wait(up_copy)
    return nt(eu_ref[...], up_ref[...])


def whole(steps):
    while True:
        try:
            next(steps)
        except StopIteration as end:
            return end.value


def together(runs):
    while runs:
        runs = [run for run in runs if next(run, "end") != "end"]


def attend_backward(*args):
    whole(attend_backward_steps(*args))


def feed_up(*args):
    return whole(feed_up_steps(*args))


def feed_back(*args):
    return whole(feed_back_steps(*args))


def rows_of(block):
    slots, _, patches, width = block.shape
    return block[:, 0].astype(F32).reshape(slots * patches, width)


def block_of(rows, ref):
    slots, _, patches, width = ref.shape
    ref[:, 0] = rows.reshape(slots, patches, width).astype(ref.dtype)


def work_shapes(tokens):
    return [
        pltpu.VMEM((4, tokens, tokens), F32),
        pltpu.VMEM((2, tokens, CHUNK), BF),
        pltpu.VMEM((4, tokens, tokens), BF),
        pltpu.VMEM((HEADS, tokens, tokens), BF),
    ]


def wide(column):
    return jnp.broadcast_to(column, (column.shape[0], LANES))


def space_steps(x, weights, state, work, arrive=lambda index: None, sent=lambda *indices: None):
    gain, w_in, w_out, scale, w_up, w_down = weights
    z0, inv0, qkv, p, o, z1, inv1, h, slope = state
    unit0, inverse0 = unit(x)
    z0[...] = unit0.astype(BF)
    inv0[...] = wide(inverse0)
    sent(0, 1)
    arrive(0)
    qkv[...] = nn((unit0 * gain[...]).astype(BF), w_in[...]).astype(BF)
    sent(2)
    yield
    yield from attend_steps(qkv, p, o, None, work[0])
    sent(3, 4)
    arrive(1)
    r1 = x + nn(o[...], w_out[...])
    unit1, inverse1 = unit(r1)
    z1[...] = unit1.astype(BF)
    inv1[...] = wide(inverse1)
    sent(5, 6)
    m = (unit1 * scale[...]).astype(BF)
    yield
    arrive(2)
    total = yield from feed_up_steps(m, w_up, w_down, h, slope, work[1])
    sent(7, 8)
    return r1 + total


def space_rows(x, weights, state, work):
    return whole(space_steps(x, weights, state, work))


def space_forward(labels, gain, scale, frames_in, w_in_in, w_out_in, w_up_in, w_down_in, *rest):
    outs, (frames, w_in, w_out, w_up, w_down), rest = rest[:10], rest[10:15], rest[15:]
    (x2, *state), (scores, u, semaphores) = rest[:10], rest[10:]
    copies = Copies(semaphores)
    packs = frames.shape[0]
    got = [
        copies.fetch(frames_in.at[pack_at(labels, pack), 0], frames.at[pack])
        for pack in range(packs)
    ]
    waits = [
        [copies.fetch(w_in_in, w_in)],
        [copies.fetch(w_out_in, w_out)],
        [copies.fetch(w_up_in, w_up), copies.fetch(w_down_in, w_down)],
    ]
    weights = gain, w_in, w_out, scale, w_up, w_down

    base = copies.count

    def leaving(index, pack):
        semaphore = semaphores.at[base + index * packs + pack]
        return pltpu.make_async_copy(state[index].at[pack], outs[1 + index].at[pack], semaphore)

    def first(pack, arrivals):
        pl.when(pack == 0)(lambda: wait(*arrivals))

    def run(pack, carry):
        def sent(*indices):
            for index in indices:
                leaving(index, pack).start()

        steps = space_steps(
            frames[pack].astype(F32),
            weights,
            [ref.at[pack] for ref in state],
            (scores, u),
            lambda index: first(pack, waits[index]),
            sent,
        )
        block_of(whole(steps), x2.at[:, pl.ds(pack, 1)])
        return carry

    wait(*got)
    lax.fori_loop(0, packs, run, 0)
    copies.count = base + len(state) * packs
    copies.send(x2, outs[0])
    for index in range(len(state)):
        for pack in range(packs):
            leaving(index, pack).wait()
    copies.finish()


def build_bias(labels, pack, slots, patches, bias):
    tokens = slots * patches
    row = lax.broadcasted_iota(jnp.int32, (1, tokens), 1)
    column = lax.broadcasted_iota(jnp.int32, (tokens, 1), 0)

    def label_of(position):
        slot = position // patches
        value = jnp.zeros_like(position)
        for f in range(slots):
            value = jnp.where(slot == f, labels[pack, f], value)
        return value

    same_patch = (row % patches) == (column % patches)
    allowed = same_patch & (column <= row) & (label_of(column) == label_of(row))
    bias[...] = jnp.where(allowed, 0.0, -1e30)


def send_moved(copies, ids, held, outs):
    if len(outs) == 1:
        copies.send(held, outs[0])
        return
    for d in range(4):
        at = 2 * (ids[1] ^ d)
        copies.send(held.at[at + ids[0]], outs[0].at[d])
        copies.send(held.at[at + 1 - ids[0]], outs[1].at[d])


def fetch_moved(copies, ids, pieces, held):
    if len(pieces) == 1:
        return [copies.fetch(pieces[0], held)]
    near, far, *others = pieces
    at = 2 * ids[1]
    got = [copies.fetch(near.at[0], held.at[at + ids[0]])]
    got.append(copies.fetch(far.at[0], held.at[at + 1 - ids[0]]))
    for d, piece in enumerate(others, 1):
        at = 2 * (ids[1] ^ d)
        got.append(copies.fetch(piece.at[0], held.at[at + ids[0]]))
        got.append(copies.fetch(piece.at[1], held.at[at + 1 - ids[0]]))
    return got


def exchange_pieces(arrays):
    if len(arrays) == 1:
        return [lax.all_to_all(arrays[0], "tm", split_axis=0, concat_axis=0, tiled=True)]
    near, far = arrays[0], swap(arrays[1], "tm", 8, 1)
    return [near, far] + [swap(jnp.stack([near[d], far[d]]), "tm", 8, 2 * d) for d in range(1, 4)]


def time_kernel(pieces, moved, labels, ids, gain, scale, x2_in, *rest):
    grad_in, rest = rest[:pieces], rest[pieces:]
    (w_in_in, w_out_in, w_up_in, w_down_in), rest = rest[:4], rest[4:]
    g0_outs, outs, rest = rest[:moved], (None,) + rest[moved : moved + 9], rest[moved + 9 :]
    x2, grad, w_in, w_out, w_up, w_down = rest[:6]
    held = rest[6:16]
    g0, out, z0, gqkv, o, e1, z1, eu, h, e2 = held
    qkv, p, slope, bias, go, scores, u, gp, gs = rest[16:25]
    copies = Copies(rest[-1])
    slots, packs, patches, _ = x2.shape
    got_x2, got_in = copies.fetch(x2_in, x2), copies.fetch(w_in_in, w_in)
    got_out, got_up = copies.fetch(w_out_in, w_out), copies.fetch(w_up_in, w_up)
    got_down, got_grad = copies.fetch(w_down_in, w_down), fetch_moved(copies, ids, grad_in, grad)

    def send(index, pack):
        copies.send(held[index].at[pack], outs[index].at[pack])

    def run(pack):
        if pack == 0:
            wait(got_x2)
        build_bias(labels, pack_at(labels, pack), slots, patches, bias.at[pack])
        x = rows_of(x2[:, pack : pack + 1])
        unit0, inverse0 = unit(x)
        z0[pack] = unit0.astype(BF)
        send(2, pack)
        if pack == 0:
            wait(got_in)
        qkv[pack] = nn((unit0 * gain[...]).astype(BF), w_in[...]).astype(BF)
        yield
        yield from attend_steps(qkv.at[pack], p.at[pack], o.at[pack], bias.at[pack], scores.at[pack])
        send(4, pack)
        if pack == 0:
            wait(got_out)
        r1 = x + nn(o[pack], w_out[...])
        unit1, inverse1 = unit(r1)
        z1[pack] = unit1.astype(BF)
        send(6, pack)
        m = (unit1 * scale[...]).astype(BF)
        yield
        if pack == 0:
            wait(got_up, got_down)
        total = yield from feed_up_steps(m, w_up, w_down, h.at[pack], slope.at[pack], u.at[pack])
        send(8, pack)
        block_of(r1 + total, out.at[:, pl.ds(pack, 1)])
        if pack == 0:
            wait(*got_grad)
        g2 = rows_of(grad[:, pack : pack + 1])
        e2[pack] = g2.astype(BF)
        send(9, pack)
        yield
        gm = yield from feed_back_steps(e2[pack], w_up, w_down, slope.at[pack], eu.at[pack])
        send(7, pack)
        g1 = g2 + unit_backward(gm * scale[...], unit1, inverse1)
        e1[pack] = g1.astype(BF)
        send(5, pack)
        go[pack] = nt(e1[pack], w_out[...]).astype(BF)
        yield
        yield from attend_backward_steps(
            qkv.at[pack], p.at[pack], go.at[pack], gqkv.at[pack], gp.at[pack], gs.at[pack]
        )
        send(3, pack)
        gn = nt(gqkv[pack], w_in[...])
        block_of(g1 + unit_backward(gn * gain[...], unit0, inverse0), g0.at[:, pl.ds(pack, 1)])

    together([run(pack) for pack in range(packs)])
    send_moved(copies, ids, g0, g0_outs)
    copies.send(out, outs[1])
    copies.finish()


def alone_both(labels, frames, grad, *rest):
    space, (gain, w_in, w_out, scale, w_up, w_down) = rest[:6], rest[6:12]
    input_grad, out = rest[12:14]
    sz0, so, se1, sgqkv, sz1, seu, sh, se2 = [ref.at[0] for ref in rest[14:22]]
    z0, o, e1, gv, z1, eu, h, e2 = [ref.at[0] for ref in rest[22:30]]
    inv0, inv1, qkv, p, sslope, slope, go, *work = rest[30:]
    state = sz0, inv0, qkv, p, so, sz1, inv1, sh, sslope
    x = space_rows(frames[0, 0].astype(F32), space, state, work)
    width = x.shape[1]
    unit0, inverse0 = unit(x)
    z0[...] = unit0.astype(BF)
    o[...] = nn((unit0 * gain[...]).astype(BF), w_in[:, 2 * width :]).astype(BF)
    r1 = x + nn(o[...], w_out[...])
    unit1, inverse1 = unit(r1)
    z1[...] = unit1.astype(BF)
    m = (unit1 * scale[...]).astype(BF)
    out[0, 0] = r1 + feed_up(m, w_up, w_down, h, slope, work[1])
    e2[...] = grad[0, 0]
    g2 = grad[0, 0].astype(F32)
    gm = feed_back(e2[...], w_up, w_down, slope, eu)
    g1 = g2 + unit_backward(gm * scale[...], unit1, inverse1)
    e1[...] = g1.astype(BF)
    gv[...] = nt(e1[...], w_out[...]).astype(BF)
    gn = nt(gv[...], w_in[:, 2 * width :])
    g2 = g1 + unit_backward(gn * gain[...], unit0, inverse0)
    gain, w_in, w_out, scale, w_up, w_down = space
    se2[...] = g2.astype(BF)
    gm = feed_back(se2[...], w_up, w_down, sslope, seu)
    g1 = g2 + unit_backward(gm * scale[...], sz1[...].astype(F32), inv1[:, :1])
    se1[...] = g1.astype(BF)
    go[...] = nt(se1[...], w_out[...]).astype(BF)
    attend_backward(qkv, p, go, sgqkv, work[2], work[3])
    gn = nt(sgqkv[...], w_in[...])
    input_grad[0, 0] = g1 + unit_backward(gn * gain[...], sz0[...].astype(F32), inv0[:, :1])


def space_back_in(labels, gqkv, w_in, gain, z0, inv0, g1, moved, input_grad, result):
    gn = nt(gqkv[0], w_in[...])
    grad = unit_backward(gn * gain[...], z0[0].astype(F32), inv0[0, :, :1])
    input_grad[0, 0] = g1[0] + grad
    result[0, 0] = rows_of(moved[...])


class Copies:
    def __init__(self, semaphores):
        self.semaphores, self.count, self.sent = semaphores, 0, []

    def fetch(self, source, target):
        copy = pltpu.make_async_copy(source, target, self.semaphores.at[self.count])
        self.count += 1
        copy.start()
        return copy

    def send(self, source, target):
        self.sent.append(self.fetch(source, target))

    def finish(self):
        for copy in self.sent:
            copy.wait()


def wait(*copies):
    for copy in copies:
        copy.wait()


def space_kernel(hierarchical, pieces, ids, scale, inv1, *rest):
    g2_in, rest = rest[:pieces], rest[pieces:]
    (slope_in, z1_in, w_out_in, w_up_in, w_down_in, qkv_in, p_in), rest = rest[:7], rest[7:]
    shared, one, rest = rest[:3], rest[3:11], rest[11:]
    (g1_out, gqkv_out), outs, scratch = rest[:2], rest[2 : 6 if hierarchical else 5], rest[6 if hierarchical else 5 :]
    g2, slope, w_out, w_up, w_down, qkv, p, go, g1, gp, gs = scratch[:11]
    z1, eu, h, e2, z0, gqkv, o, e1 = whole = scratch[11:19]
    copies = Copies(scratch[-1])
    packs, tokens, _ = g1.shape
    have = packs * tokens
    got_g2 = fetch_moved(copies, ids, g2_in, g2)
    got_down = copies.fetch(w_down_in, w_down)
    got_slope = [copies.fetch(slope_in.at[pack], slope.at[pack]) for pack in range(packs)]
    got_up = copies.fetch(w_up_in, w_up)
    got_z1 = [
        copies.fetch(z1_in.at[pack], z1.at[pl.ds(pack * tokens, tokens)]) for pack in range(packs)
    ]
    got_out = copies.fetch(w_out_in, w_out)
    got_attend = [
        (copies.fetch(qkv_in.at[pack], qkv.at[pack]), copies.fetch(p_in.at[pack], p.at[pack]))
        for pack in range(packs)
    ]
    got_rest = []
    if hierarchical:
        for source, target in zip(shared, (h, z0, o)):
            for pack in range(packs):
                rows = pl.ds(pack * tokens, tokens)
                got_rest.append(copies.fetch(source.at[pack], target.at[rows]))
        for source, target in zip(one, whole):
            got_rest.append(copies.fetch(source.at[0], target.at[pl.ds(have, tokens)]))
    wait(*got_g2)

    def run(pack):
        rows = slice(pack * tokens, (pack + 1) * tokens)
        e2[rows] = rows_of(g2[:, pack : pack + 1]).astype(BF)
        if pack == 0:
            wait(got_down)
        wait(got_slope[pack])
        gm = yield from feed_back_steps(e2[rows], w_up, w_down, slope.at[pack], eu.at[rows], got_up if pack == 0 else None)
        if pack == 0:
            wait(*got_z1, got_out)
        grad = unit_backward(gm * scale[...], z1[rows].astype(F32), inv1[pack, :, :1])
        total = rows_of(g2[:, pack : pack + 1]) + grad
        g1[pack] = total
        e1[rows] = total.astype(BF)
        go[pack] = nt(e1[rows], w_out[...]).astype(BF)
        copies.send(g1.at[pack], g1_out.at[pack])
        yield
        wait(*got_attend[pack])
        rows = pl.ds(pack * tokens, tokens)
        yield from attend_backward_steps(
            qkv.at[pack], p.at[pack], go.at[pack], gqkv.at[rows], gp.at[pack], gs.at[pack]
        )
        copies.send(gqkv.at[rows], gqkv_out.at[pack])

    together([run(pack) for pack in range(packs)])
    if hierarchical:
        wait(*got_rest)
        one = Halves(copies, ids, scratch[19:21], outs[:2], x_high=True)
        two = Halves(copies, ids, scratch[21:23], outs[2:])
        up_tiles(one, z1, eu, 0)
        down_tiles(two, e2, h, 0)
        attend_tiles([one, one, two, two], z0, o, gqkv, e1, [64, 80, 64, 80], gqkv.shape[0])
    else:
        for source, target in zip((eu, e2, e1), outs):
            copies.send(source, target)
    copies.finish()


def to_send(labels, ids, grad, *rest):
    *outs, held = rest
    slots, places, patches, _ = held.shape
    for place in range(places):
        rows = grad[pack_at(labels, place), 0].astype(F32)
        held[:, place] = rows.reshape(slots, patches, -1).astype(BF)
    if len(outs) == 1:
        outs[0][...] = held[...]
        return
    for d in range(4):
        at = 2 * (ids[1] ^ d)
        outs[0][d] = held[at + ids[0]]
        outs[1][d] = held[at + 1 - ids[0]]


def pack_at(labels, place):
    packs, slots = labels.shape
    alone = packs - 1
    for pack in range(packs - 2, -1, -1):
        alone = jnp.where(labels[pack, slots - 1] == slots - 1, pack, alone)
    return jnp.where(place == packs - 1, alone, place + (place >= alone).astype(jnp.int32))


def without(kernel, first, count):
    def call(*refs):
        return kernel(*refs[:first], *refs[first + count :])

    return call


class Packs:
    def __init__(self, labels, first, count):
        self.labels, self.first, self.count = labels, first, count

    def call(self, kernel, args, outs, scratch=(), flops=0, after=()):
        first, last = self.first, self.labels.shape[0] - 2
        scalars = (self.labels,)

        def spec(kind, shape):
            rank = len(shape)
            if kind == "whole":
                return pl.BlockSpec(shape, lambda i, *s: (0,) * rank)
            if kind == "pack":
                return pl.BlockSpec(
                    (1,) + tuple(shape[1:]), lambda i, s: (pack_at(s, first + i),) + (0,) * (rank - 1)
                )
            if kind == "place":
                return pl.BlockSpec(
                    (1,) + tuple(shape[1:]), lambda i, *s: (first + i,) + (0,) * (rank - 1)
                )
            if kind == "step":
                return pl.BlockSpec(
                    (1,) + tuple(shape[1:]), lambda i, *s: (i,) + (0,) * (rank - 1)
                )
            if kind == "moved":
                return pl.BlockSpec(
                    (shape[0], 1, shape[2], shape[3]),
                    lambda i, *s: (0, jnp.minimum(i, last), 0, 0),
                )
            return pl.BlockSpec(memory_space=pl.ANY)

        in_specs = [spec(kind, array.shape) for kind, array in args]
        operands = [array for _, array in args]
        aliases = {}
        for index, (kind, shape, dtype, into) in enumerate(outs):
            if into is not None:
                aliases[len(scalars) + len(operands)] = index
                operands.append(into)
                in_specs.append(pl.BlockSpec(memory_space=pl.ANY))
        for array in after:
            operands.append(array)
            in_specs.append(pl.BlockSpec(memory_space=pl.ANY))
        moved = sum(a.size * a.dtype.itemsize for a in operands)
        unread = len(operands) - len(args)
        return pl.pallas_call(
            without(kernel, len(scalars) + len(args), unread),
            out_shape=[jax.ShapeDtypeStruct(shape, dtype) for _, shape, dtype, _ in outs],
            grid_spec=pltpu.PrefetchScalarGridSpec(
                num_scalar_prefetch=len(scalars),
                grid=(self.count,),
                in_specs=in_specs,
                out_specs=[spec(kind, shape) for kind, shape, _, _ in outs],
                scratch_shapes=list(scratch),
            ),
            input_output_aliases=aliases,
            compiler_params=pltpu.CompilerParams(
                vmem_limit_bytes=VMEM, dimension_semantics=("arbitrary",)
            ),
            cost_estimate=pl.CostEstimate(
                flops=int(flops * self.count * COST), bytes_accessed=int(moved * COST), transcendentals=0
            ),
        )(*scalars, *operands)


class Halves:
    def __init__(self, copies, ids, held, outs, x_high=False):
        self.copies, self.held, self.outs = copies, held, outs
        self.first, self.z, self.s, self.x_high = ids[0] == 0, ids[1], ids[2], x_high

    def part(self, s):
        if s is None:
            return slice(None)
        part = s ^ self.s
        return (part & 1) * 2 + (part >> 1) if self.x_high else part

    def put(self, s, z, at, even, odd):
        rows = slice(at, at + even.shape[0])
        self.held[0][self.part(s), z ^ self.z, rows] = jnp.where(self.first, even, odd)
        self.held[1][self.part(s), z ^ self.z, rows] = jnp.where(self.first, odd, even)

    def send(self, s, z, at, rows):
        index = self.part(s), slice(None) if z is None else z ^ self.z, pl.ds(at, rows)
        for ref, out in zip(self.held, self.outs):
            self.copies.send(ref.at[index], out.at[index])


def up_tiles(place, z1, eu, at):
    for step in range(4):
        tile = tn(z1[...], eu[:, step * CHUNK : (step + 1) * CHUNK]).astype(BF)
        for z in range(4):
            row = 128 * z
            place.put(step, z, at, tile[row : row + 64], tile[row + 64 : row + 128])
        place.send(step, None, at, 64)


def down_tiles(place, e2, h, at):
    for step in range(4):
        tile = tn(e2[...], h[:, step * CHUNK : (step + 1) * CHUNK]).astype(BF)
        for s in range(4):
            upper, lower = tile[128 * s : 128 * s + 64], tile[128 * s + 64 : 128 * s + 128]
            even = jnp.concatenate([upper[:, :256], lower[:, :256]], axis=1)
            odd = jnp.concatenate([upper[:, 256:], lower[:, 256:]], axis=1)
            place.put(s, step, at, even, odd)
        place.send(None, step, at, 64)


def attend_tiles(places, z0, o, gqkv, e1, ats, depth):
    for step, (place, at) in enumerate(zip(places, ats)):
        if step == 3:
            tile = tn(o[...], e1[...])
        else:
            rows = gqkv.shape[0] if step == 2 else depth
            tile = tn(z0[:rows], gqkv[:rows, step * CHUNK : (step + 1) * CHUNK])
        tile = tile.astype(BF)
        for z in range(4):
            for s in range(4):
                row = 128 * z + 16 * s
                place.put(s, z, at, tile[row : row + 16], tile[row + 64 : row + 80])
        if step % 2:
            place.send(None, None, at - 16, 32)


def time_weights_kernel(ids, *rest):
    names = 8
    shared, single, outs, scratch = rest[:names], rest[names : 2 * names], rest[16:20], rest[20:]
    z1, eu, e2, h, z0, gqkv, o, e1 = scratch[:names]
    copies = Copies(scratch[-1])
    one = Halves(copies, ids, scratch[8:10], outs[:2], x_high=True)
    two = Halves(copies, ids, scratch[10:12], outs[2:])
    packs, tokens, _ = shared[0].shape
    have = packs * tokens
    got = []
    for source, last, target in zip(shared, single, scratch):
        wide_target = target.at[pl.ds(have, tokens)]
        if last.shape[2] < target.shape[1]:
            wide_target = target.at[pl.ds(have, tokens), pl.ds(target.shape[1] - last.shape[2], last.shape[2])]
        got.append(
            [copies.fetch(source.at[pack], target.at[pl.ds(pack * tokens, tokens)]) for pack in range(packs)]
            + [copies.fetch(last.at[0], wide_target)]
        )
    wait(*got[0], *got[1], *got[2], *got[3])
    up_tiles(one, z1, eu, 0)
    down_tiles(two, e2, h, 0)
    wait(*got[4], *got[5], *got[6], *got[7])
    attend_tiles([one, one, two, two], z0, o, gqkv, e1, [64, 80, 64, 80], have)
    copies.finish()


def manual_call(kernel, ids, args, outs, scratch, semaphores, small=0, after=(), flops=0):
    anywhere = pl.BlockSpec(memory_space=pl.ANY)
    scalars = ids if isinstance(ids, tuple) else (ids,)
    return pl.pallas_call(
        without(kernel, len(scalars) + len(args), len(after)),
        out_shape=[jax.ShapeDtypeStruct(shape, dtype) for shape, dtype in outs],
        in_specs=[pl.BlockSpec(memory_space=pltpu.SMEM)] * len(scalars)
        + [pl.BlockSpec(memory_space=pltpu.VMEM)] * small
        + [anywhere] * (len(args) - small + len(after)),
        out_specs=[anywhere] * len(outs),
        scratch_shapes=[pltpu.VMEM(shape, dtype) for shape, dtype in scratch]
        + [pltpu.SemaphoreType.DMA((semaphores,))],
        compiler_params=pltpu.CompilerParams(vmem_limit_bytes=VMEM),
        cost_estimate=pl.CostEstimate(
            flops=int(flops * COST), bytes_accessed=0, transcendentals=0
        ),
    )(*scalars, *args, *after)


def swap(array, axis, size, mask):
    return lax.ppermute(array, axis, [(i, i ^ mask) for i in range(size)])


def add(*terms):
    total = terms[0].astype(F32)
    for term in terms[1:]:
        total = total + term.astype(F32)
    return total.astype(BF)


def far_parts(mine, got, note):
    return [add(a[2:], b[2:], note) for a, b in zip(mine, got)]


def near_parts(mine, got, far):
    halves = [swap(far[0], "stream", 4, 1), swap(far[1], "stream", 4, 2)]
    return halves, [add(a[1], b[1], half[1]) for a, b, half in zip(mine, got, halves)]


def stream_rows(mine, got, halves, near, *note):
    last = [swap(near[0], "stream", 4, 2), swap(near[1], "stream", 4, 1)]
    terms = list(zip(mine, got, halves, last))
    return [
        jnp.concatenate([add(a[0][d], b[0][d], half[0][d], end[d], *note) for a, b, half, end in terms])
        for d in range(4)
    ]


def z_got(rows):
    return [swap(rows[d], "tm", 8, 2 * d) for d in range(1, 4)]


def z_sum(rows):
    return add(rows[0], *[swap(rows[d], "tm", 8, 2 * d) for d in range(1, 4)])


def gather_parts(final):
    return [final] + [swap(final, "stream", 4, d) for d in range(1, 4)]


def marker(*arrays):
    def kernel(*refs):
        refs[-1][...] = jnp.zeros_like(refs[-1])

    return pl.pallas_call(
        kernel,
        out_shape=jax.ShapeDtypeStruct((1, CHUNK), F32),
        in_specs=[pl.BlockSpec(memory_space=pl.ANY)] * len(arrays),
        out_specs=pl.BlockSpec(memory_space=pltpu.VMEM),
        cost_estimate=pl.CostEstimate(flops=10**12, bytes_accessed=10**8, transcendentals=0),
    )(*arrays)


def as_row(col):
    size = col.shape[0]
    eye = lax.broadcasted_iota(jnp.int32, (size, size), 0) == lax.broadcasted_iota(
        jnp.int32, (size, size), 1
    )
    return jnp.sum(jnp.where(eye, col, 0.0), axis=0, keepdims=True)


def own_rows(ids, vector):
    shape = 64, vector.shape[1]
    row = lax.broadcasted_iota(jnp.int32, shape, 0) + 64 * (2 * ids[1] + ids[0])
    lane = lax.broadcasted_iota(jnp.int32, shape, 1)
    return jnp.sum(jnp.where(row == lane, vector[...], 0.0), axis=1, keepdims=True)


def finish_kernel(ids, p0, p1, p2, p3, w_up, scale, w_in, gain, *outs):
    scale_grad, up_grad, down_grad, gain_grad, in_grad, out_grad = outs
    up_at, down_at, *in_at, out_at = ROWS
    for d, piece in enumerate((p0, p1, p2, p3)):
        s = ids[2] ^ d
        up_grad[:, pl.ds(pl.multiple_of(512 * s, 512), 512)] = piece[up_at : up_at + 64].astype(F32)
        lower = piece[down_at : down_at + 64].astype(F32)
        whole = jnp.concatenate([lower[:, :256], lower[:, 256:]], axis=0)
        down_grad[:, pl.ds(pl.multiple_of(128 * s, 128), 128)] = whole.T
        rows = pl.ds(pl.multiple_of(16 * s, 16), 16)
        for third, at in enumerate(in_at):
            in_grad[rows, 512 * third : 512 * third + 512] = piece[at : at + 16].astype(F32)
        out_grad[rows, :] = piece[out_at : out_at + 16].astype(F32)
    for grad, weight, factor, vector_grad in (
        (up_grad, w_up, scale, scale_grad),
        (in_grad, w_in, gain, gain_grad),
    ):
        total = grad[...]
        vector_grad[...] = as_row(jnp.sum(total * weight[...].astype(F32), axis=1, keepdims=True))
        grad[...] = total * own_rows(ids, factor)


def finish_call(kernel, ids, pieces, pairs, outs):
    whole = pl.BlockSpec(pieces[0].shape, lambda i, *s: (0, 0))
    specs, operands = [], []
    for weight, vector in pairs:
        height = weight.shape[0] // 8
        specs += [
            pl.BlockSpec((height, weight.shape[1]), lambda i, s: (2 * s[1] + s[0], 0)),
            pl.BlockSpec((1, vector.size), lambda i, *s: (0, 0)),
        ]
        operands += [weight, vector.reshape(1, -1)]
    results = pl.pallas_call(
        kernel,
        out_shape=[jax.ShapeDtypeStruct(shape, F32) for shape in outs],
        grid_spec=pltpu.PrefetchScalarGridSpec(
            num_scalar_prefetch=1,
            grid=(1,),
            in_specs=[whole] * 4 + specs,
            out_specs=[pl.BlockSpec(shape, lambda i, *s: (0, 0)) for shape in outs],
        ),
        compiler_params=pltpu.CompilerParams(vmem_limit_bytes=SMALL_VMEM),
    )(ids, *pieces, *operands)
    return [a.reshape(-1) if a.shape[0] == 1 else a for a in results]


def plain_grads(z, grads, left, right, weight, vector):
    product = tn(z, grads)
    vector_grad = jnp.sum(product * weight.astype(F32), axis=1)
    sums = []
    for term in (vector_grad, product * vector[:, None], tn(left, right)):
        share = lax.psum_scatter(term.astype(BF), "tm", scatter_dimension=0, tiled=True)
        sums.append(lax.psum(share, "stream").astype(F32))
    return sums


def grad_to_send(labels, ids, grad, shape, outs):
    space = pl.BlockSpec(memory_space=pltpu.VMEM)
    return pl.pallas_call(
        to_send,
        out_shape=[jax.ShapeDtypeStruct(shape, dtype) for shape, dtype in outs],
        in_specs=[pl.BlockSpec(memory_space=pltpu.SMEM)] * 2 + [space],
        out_specs=[space] * len(outs),
        scratch_shapes=[pltpu.VMEM(shape, BF)],
        compiler_params=pltpu.CompilerParams(vmem_limit_bytes=VMEM),
    )(labels, ids, grad)


def per_device(
    ranks,
    streams,
    frames,
    space_gain,
    space_input,
    space_output,
    space_scale,
    space_up,
    space_down,
    time_gain,
    time_input,
    time_output,
    time_scale,
    time_up,
    time_down,
    clip_labels,
    output_grad,
):
    packs, _, tokens, width = frames.shape
    slots = clip_labels.shape[1]
    patches = tokens // ranks
    hidden = space_up.shape[1]
    some = packs - 1
    hierarchical = (ranks, streams) == (8, 4)
    tm = lax.axis_index("tm")
    ids = jnp.stack([tm % 2, tm // 2, lax.axis_index("stream")]).astype(jnp.int32)
    shared = Packs(clip_labels, 0, some)
    single = Packs(clip_labels, some, 1)

    def row(vector):
        return vector.reshape(1, -1)

    def exchange(array):
        return lax.all_to_all(array, "tm", split_axis=0, concat_axis=0, tiled=True)

    def steps(count, *tails):
        return [("step", (count,) + tail, BF, None) for tail in tails]

    moved = ("moved", (slots, some, patches, width), BF, None)
    whole = ("pack", frames.shape, F32, None)
    flops = 2 * tokens * width * (4 * width + 2 * hidden)

    shape = moved[1]
    halves = (slots // 2,) + shape[1:]
    moved_outs = [(halves, BF)] * 2 if hierarchical else [(shape, BF)]
    sent = grad_to_send(clip_labels, ids, output_grad, shape, moved_outs)
    grad_moved = exchange_pieces(sent)

    space_args = [
        ("whole", row(space_gain)),
        ("whole", space_input),
        ("whole", space_output),
        ("whole", row(space_scale)),
        ("whole", space_up),
        ("whole", space_down),
    ]
    time_args = [
        ("whole", row(time_gain)),
        ("whole", time_input),
        ("whole", time_output),
        ("whole", row(time_scale)),
        ("whole", time_up),
        ("whole", time_down),
    ]
    rows_w, rows_3, rows_h = (tokens, width), (tokens, 3 * width), (tokens, hidden)
    shared_w, shared_3, shared_h = [(some,) + tail for tail in (rows_w, rows_3, rows_h)]
    square, spread = (some, HEADS, tokens, tokens), (some, tokens, LANES)
    space_outs = [
        (shape, BF),
        (shared_w, BF),
        (spread, F32),
        (shared_3, BF),
        (square, BF),
        (shared_w, BF),
        (shared_w, BF),
        (spread, F32),
        (shared_h, BF),
        (shared_h, BF),
    ]
    x2, sz0, sinv0, sqkv, sp, so, sz1, sinv1, sh, sslope = manual_call(
        space_forward,
        clip_labels,
        [row(space_gain), row(space_scale), frames]
        + [space_input, space_output, space_up, space_down],
        space_outs,
        [(shared_w, BF)]
        + [(w.shape, BF) for w in (space_input, space_output, space_up, space_down)]
        + space_outs
        + [((4, tokens, tokens), F32), ((2, tokens, CHUNK), BF)],
        5 + 10 * some,
        small=2,
        after=sent,
        flops=some * flops,
    )
    x2_moved = exchange(x2)
    held_back = grad_moved
    if hierarchical:
        held_back = [marker(*grad_moved[2:])]

    block_tails = [rows_w, rows_w, rows_w, rows_3, rows_w, rows_h, rows_h, rows_w]
    time_tails = [rows_w, rows_w, rows_w, rows_w, rows_w, rows_h, rows_h, rows_w]
    input_grad, result, *alone = single.call(
        alone_both,
        [("pack", frames), ("pack", output_grad)] + space_args + time_args,
        [whole, whole] + steps(1, *block_tails) + steps(1, *time_tails),
        scratch=[
            pltpu.VMEM((tokens, LANES), F32),
            pltpu.VMEM((tokens, LANES), F32),
            pltpu.VMEM(rows_3, BF),
            pltpu.VMEM((HEADS, tokens, tokens), BF),
            pltpu.VMEM(rows_h, BF),
            pltpu.VMEM(rows_h, BF),
            pltpu.VMEM(rows_w, BF),
        ]
        + work_shapes(tokens),
        flops=6 * flops,
        after=(x2, *held_back),
    )
    sz0_one, so_one, se1_one, sgqkv_one, sz1_one, seu_one, sh_one, se2_one = alone[:8]
    tz0_one, to_one, te1_one, tgv_one, tz1_one, teu_one, th_one, te2_one = alone[8:]

    time_outs = [(x2.shape, BF)] * 2 + [
        (shape, BF)
        for shape in (shared_w, shared_3, shared_w, shared_w, shared_w, shared_h, shared_h, shared_w)
    ]
    *g0, out, tz0, tgqkv, to, te1, tz1, teu, th, te2 = manual_call(
        functools.partial(time_kernel, len(grad_moved), len(moved_outs)),
        (clip_labels, ids),
        [row(time_gain), row(time_scale), x2_moved, *grad_moved]
        + [time_input, time_output, time_up, time_down],
        moved_outs + time_outs[1:],
        [(x2.shape, BF)] * 2
        + [(w.shape, BF) for w in (time_input, time_output, time_up, time_down)]
        + time_outs
        + [
            (shared_3, BF),
            (square, BF),
            (shared_h, BF),
            ((some, tokens, tokens), F32),
            (shared_w, BF),
            ((some, 4, tokens, tokens), F32),
            ((some, 2, tokens, CHUNK), BF),
            ((some, 4, tokens, tokens), BF),
            (square, BF),
        ],
        14 + 8 * some + 9,
        small=2,
        after=(sz0_one,),
        flops=3 * some * flops,
    )
    g0_moved = exchange_pieces(g0)
    out, g0_moved = lax.optimization_barrier((out, g0_moved))
    out_moved = exchange(out)

    held_back = ()
    everything = packs * tokens
    feed_shapes = [(1, width // 8), (width // 8, hidden), (hidden // 8, width)]
    attend_shapes = [(1, width // 8), (width // 8, 3 * width), (width // 8, width)]
    time_shared = [tz1, teu, te2, th, tz0, tgqkv, to, te1]
    time_one = [tz1_one, teu_one, te2_one, th_one, tz0_one, tgv_one, to_one, te1_one]
    if hierarchical:
        parts_shapes = [((4, 4, 96, CHUNK), BF)] * 4
        time_terms = manual_call(
            time_weights_kernel,
            ids,
            time_shared + time_one,
            parts_shapes,
            [((everything, a.shape[2]), BF) for a in time_shared] + parts_shapes,
            8 * packs + 20,
            flops=packs * flops,
        )
        time_got = [swap(other, "tm", 8, 1) for other in time_terms[1::2]]
        time_far = far_parts(time_terms[::2], time_got, marker(*g0_moved[2:]))
        held_back = time_far
    else:
        grad_one = jnp.pad(tgv_one, ((0, 0), (0, 0), (2 * width, 0)))
        joined = [joint(a, b) for a, b in zip(time_shared, time_one[:5] + [grad_one] + time_one[6:])]
        time_grads = plain_grads(joined[0], joined[1], joined[3], joined[2], time_up, time_scale)
        time_grads += plain_grads(joined[4], joined[5], joined[6], joined[7], time_input, time_gain)

    space_one = [sz1_one, seu_one, sh_one, se2_one, sz0_one, sgqkv_one, so_one, se1_one]
    whole_shapes = [((everything, a.shape[2]), BF) for a in space_one]
    parts_shapes = [((4, 4, 96, CHUNK), BF)] * 4
    sg1, sgqkv, *weights = manual_call(
        functools.partial(space_kernel, hierarchical, len(g0_moved)),
        ids,
        [row(space_scale), sinv1, *g0_moved, sslope, sz1, space_output, space_up, space_down]
        + [sqkv, sp, sh, sz0, so]
        + space_one,
        [(shared_w, F32), (shared_3, BF)]
        + (parts_shapes if hierarchical else [whole_shapes[i] for i in (1, 3, 7)]),
        [
            (x2.shape, BF),
            (sslope.shape, BF),
            (space_output.shape, BF),
            (space_up.shape, BF),
            (space_down.shape, BF),
            (sqkv.shape, BF),
            (sp.shape, BF),
            (shared_w, BF),
            (shared_w, F32),
            ((some, 4, tokens, tokens), BF),
            (square, BF),
        ]
        + whole_shapes
        + (parts_shapes if hierarchical else []),
        96,
        small=2,
        after=held_back,
        flops=2 * packs * flops,
    )
    held_back = ()
    if hierarchical:
        time_got, sgqkv = lax.optimization_barrier((time_got, sgqkv))
        time_mine = time_terms[::2]
        time_halves, time_near = near_parts(time_mine, time_got, time_far)
        mine = weights[::2]
        got = [swap(other, "tm", 8, 1) for other in weights[1::2]]
        far = far_parts(mine, got, marker(time_near[1]))
        held_back = far
    input_grad, result = shared.call(
        space_back_in,
        [
            ("step", sgqkv),
            ("whole", space_input),
            ("whole", row(space_gain)),
            ("step", sz0),
            ("step", sinv0),
            ("step", sg1),
            ("moved", out_moved),
        ],
        [("pack", frames.shape, F32, input_grad), ("pack", frames.shape, F32, result)],
        flops=flops // 4,
        after=held_back,
    )
    if hierarchical:
        time_halves, input_grad = lax.optimization_barrier((time_halves, input_grad))
        time_rows = stream_rows(time_mine, time_got, time_halves, time_near)
        time_last = z_got(time_rows)
        time_final = add(time_rows[0], *time_last)
        final = z_sum(stream_rows(mine, got, *near_parts(mine, got, far), marker(*time_last)))
        grads = finish_call(
            finish_kernel,
            ids,
            gather_parts(final),
            [(space_up, space_scale), (space_input, space_gain)],
            feed_shapes + attend_shapes,
        )
        feed_grads, attend_grads = grads[:3], grads[3:]
        time_grads = finish_call(
            finish_kernel,
            ids,
            gather_parts(time_final),
            [(time_up, time_scale), (time_input, time_gain)],
            feed_shapes + attend_shapes,
        )
    else:
        have = some * tokens
        seu, se2, se1 = [a[:have].reshape(some, tokens, -1) for a in weights]
        feed_grads = plain_grads(
            joint(sz1, sz1_one),
            joint(seu, seu_one),
            joint(sh, sh_one),
            joint(se2, se2_one),
            space_up,
            space_scale,
        )
        attend_grads = plain_grads(
            joint(sz0, sz0_one),
            joint(sgqkv, sgqkv_one),
            joint(so, so_one),
            joint(se1, se1_one),
            space_input,
            space_gain,
        )
    grads = attend_grads + feed_grads + time_grads[3:] + time_grads[:3]
    return (result, input_grad, *grads)


def joint(shared, one):
    return jnp.concatenate([shared, one]).reshape(-1, shared.shape[-1])


def solution(mesh):
    tokens = P("stream", "tm", None, None)
    vector, matrix = P("tm"), P("tm", None)
    return jax.shard_map(
        functools.partial(per_device, mesh.shape["tm"], mesh.shape["stream"]),
        mesh=mesh,
        in_specs=(tokens,) + (P(),) * 12 + (P("stream", None), tokens),
        out_specs=(tokens, tokens) + (vector, matrix, matrix, vector, matrix, matrix) * 2,
        check_vma=False,
    )
```

profile of v0, /device:TPU:16, one launch (start us, length us, event | category | flops | bytes accessed | tf_op | source)
XLA Modules:
  0.0 213.1 jit_solution(4680575272353171842)
XLA Ops:
  1.3 2.2 %shard_map.254 = (bf16[4,3,32,512]{3,2,1,0:T(8,128)(2,1)}, bf16[4,3,32,512]{3,2,1,0:T(8,128)(2,1)}) custom-call(s32[4,8]{1,0:T(4,128)} %refs_0_.7, s32[3]{0:T(128)} %pad_add_fusion.ids.refs_1_.refs_0_, bf16[4,1,256,512]{3,2,1,0:T(8,128)(2,1)} %refs_2_.2), custom_call_target="tpu_custom_call" | custom-call | tf_op jit(solution)/shard_map/pallas_call | solution.py:883
  5.5 1.6 collective-permute-start.1
  7.6 1.6 collective-permute-start.3
  9.2 14.7 %shard_map.255 = (bf16[8,3,32,512]{3,2,1,0:T(8,128)(2,1)}, bf16[3,256,512]{2,1,0:T(8,128)(2,1)}, f32[3,256,128]{2,1,0:T(8,128)}, bf16[3,256,1536]{2,1,0:T(8,128)...) custom-call(s32[4,8]{1,0:T(4,128)} %refs_0_.7, ...), custom_call_target="tpu_custom_call" | custom-call | flops 4831838208 | tf_op jit(solution)/shard_map/pallas_call | solution.py:740
  24.0 6.3 %all-to-all-start = ((bf16[8,3,32,512]{3,2,1,0:T(8,128)(2,1)}), bf16[8,3,32,512]{3,2,1,0:T(8,128)(2,1)}, u32[]{:S(2)}, u32[]{:S(2)}) async-start(bf16[8,3,32,512]{3,2,1,0:T(8,128)(2,1)} %get-tuple-element.93.refs_15_), calls=%async_computation | async-start | bytes 1572864 | tf_op jit(solution)/shard_map/all_to_all | solution.py:927
  32.2 18.8 %shard_map.257 = (f32[4,1,256,512]{3,2,1,0:T(8,128)}, f32[4,1,256,512]{3,2,1,0:T(8,128)}, bf16[1,256,512]{2,1,0:T(8,128)(2,1)}, bf16[1,256,512]{2,1,0:T(8,128)(2...) custom-call(s32[4,8]{1,0:T(4,128)} %refs_0_.7, ...), custom_call_target="tpu_custom_call" | custom-call | flops 9663676416 | bytes 15476736 | tf_op jit(solution)/shard_map/pallas_call | solution.py:633
  51.1 23.3 %shard_map.258 = (bf16[4,3,32,512]{3,2,1,0:T(8,128)(2,1)}, bf16[4,3,32,512]{3,2,1,0:T(8,128)(2,1)}, bf16[8,3,32,512]{3,2,1,0:T(8,128)(2,1)}, bf16[3,256,512]{2,1...) custom-call(s32[4,8]{1,0:T(4,128)} %refs_0_.7, ...), custom_call_target="tpu_custom_call" | custom-call | flops 14495514624 | tf_op jit(solution)/shard_map/pallas_call | solution.py:740
  80.2 13.1 %shard_map.259 = (bf16[4,4,96,512]{3,2,1,0:T(8,128)(2,1)}, bf16[4,4,96,512]{3,2,1,0:T(8,128)(2,1)}, bf16[4,4,96,512]{3,2,1,0:T(8,128)(2,1)}, bf16[4,4,96,512]{3,2,1,0:T(8,128)(2,1)}) custom-call(s32[3]{0:T(128)} %pad_add_fusion.ids.refs_1_.refs_0_, bf16[3,256,512]{2,1,0:T(8,128)(2,1)} %get-tuple-element.95.refs_1_, ...), custom_call_target="tpu_custom_call" | custom-call | flops 6442450944 | tf_op jit(solution)/shard_map/pallas_call | solution.py:740
  93.9 3.6 %collective-permute-done.9.refs_2_.refs_7_ = bf16[2,3,32,512]{3,2,1,0:T(8,128)(2,1)S(1)} collective-permute-done((bf16[2,3,32,512]{3,2,1,0:T(8,128)(2,1)S(1)}, bf16[2,3,32,512]{3,2,1,0:T(8,128)(2,1)S(1)}, u32[]{:S(2)}, u32[]{:S(2)}) %collective-permute-start.9) | collective-permute-done | bytes 196640 | tf_op jit(solution)/shard_map/ppermute | solution.py:757
  98.1 4.3 %all-to-all-start.1 = ((bf16[8,3,32,512]{3,2,1,0:T(8,128)(2,1)}), bf16[8,3,32,512]{3,2,1,0:T(8,128)(2,1)}, u32[]{:S(2)}, u32[]{:S(2)}) async-start(bf16[8,3,32,512]{3,2,1,0:T(8,128)(2,1)} %get-tuple-element.142), calls=%async_computation.1 | async-start | bytes 1572864 | tf_op jit(solution)/shard_map/all_to_all | solution.py:927
  104.4 3.0 %add_convert_fusion.2 = (bf16[2,4,96,512]{3,2,1,0:T(8,128)(2,1)}, bf16[2,4,96,512]{3,2,1,0:T(8,128)(2,1)}) fusion(bf16[4,4,96,512]{3,2,1,0:T(8,128)(2,1)} %collective-permute-done.5, bf16[4,4,96,512]{3,2,1,0:T(8,128)(2,1)S(1)} %copy-done.13, f32[512]{0:T(512)} %bitcast.151, bf16[4,4,96,512]{3,2,1,0:T(8,128)(2,1)} %collective-permute-done.4, ...), kind=kLoop, calls=%fused_computation.2 | loop fusion | flops 3932160 | bytes 4720640 | tf_op jit(solution)/shard_map/convert_element_type | solution.py:764
  110.4 21.2 %shard_map.261 = (f32[3,256,512]{2,1,0:T(8,128)}, bf16[3,256,1536]{2,1,0:T(8,128)(2,1)}, bf16[4,4,96,512]{3,2,1,0:T(8,128)(2,1)}, bf16[4,4,96,512]{3,2,1,0:T(8,1...) custom-call(s32[3]{0:T(128)} %pad_add_fusion.ids.refs_1_.refs_0_, f32[1,512]{1,0:T(1,128)} %bitcast.146, ...), custom_call_target="tpu_custom_call" | custom-call | flops 12884901888 | tf_op jit(solution)/shard_map/pallas_call | solution.py:740
  132.2 2.2 %fusion.refs_0_ = bf16[4,96,512]{2,1,0:T(8,128)(2,1)} fusion(bf16[2,4,96,512]{3,2,1,0:T(8,128)(2,1)S(1)} %collective-permute-done.11, bf16[4,4,96,512]{3,2,1,0:T(8,128)(2,1)} %collective-permute-done.5, bf16[4,4,96,512]{3,2,1,0:T(8,128)(2,1)S(1)} %copy-done.13), kind=kLoop, calls=%fused_computation.8 | loop fusion | flops 1179648 | bytes 1572864 | tf_op jit(solution)/shard_map/convert_element_type | solution.py:764
  137.7 2.1 add_convert_fusion
  142.7 7.4 %shard_map.263 = (f32[4,1,256,512]{3,2,1,0:T(8,128)}, f32[4,1,256,512]{3,2,1,0:T(8,128)}) custom-call(s32[4,8]{1,0:T(4,128)} %refs_0_.7, bf16[3,256,1536]{2,1,0:T(8,128)(2,1)} %get-tuple-element.139.refs_1_, bf16[512,1536]{1,0:T(8,128)(2,1)} %w_in.2, f32[1,512]{1,0:T(1,128)} %bitcast.136, ...), custom_call_target="tpu_custom_call", output_to_operand_aliasing={{0}: (8, {}), {1}: (9, {})} | custom-call | flops 1207959552 | bytes 13240320 | tf_op jit(solution)/shard_map/pallas_call | solution.py:633
  150.0 2.3 %fusion.4 = (bf16[96,512]{1,0:T(8,128)(2,1)}, bf16[96,512]{1,0:T(8,128)(2,1)S(1)}, bf16[96,512]{1,0:T(8,128)(2,1)S(1)}, bf16[96,512]{1,0:T(8,128)(2,1)S(1)}) fusion(bf16[4,96,512]{2,1,0:T(8,128)(2,1)} %collective-permute-done.17, bf16[2,4,96,512]{3,2,1,0:T(8,128)(2,1)} %copy-done.14, bf16[4,4,96,512]{3,2,1,0:T(8,128)(2,1)} %collective-permute-done.5, ...), kind=kLoop, calls=%fused_computation.27 | loop fusion | flops 1572864 | bytes 1966080 | tf_op jit(solution)/shard_map/convert_element_type | solution.py:764
  152.4 2.3 %fusion.5 = (bf16[96,512]{1,0:T(8,128)(2,1)}, bf16[96,512]{1,0:T(8,128)(2,1)S(1)}, bf16[96,512]{1,0:T(8,128)(2,1)S(1)}, bf16[96,512]{1,0:T(8,128)(2,1)S(1)}) fusion(bf16[4,96,512]{2,1,0:T(8,128)(2,1)} %collective-permute-done.16, bf16[2,4,96,512]{3,2,1,0:T(8,128)(2,1)} %collective-permute-done.13, bf16[4,4,96,512]{3,2,1,0:T(8,128)(2,1)} %collective-permute-done.4, ...), kind=kLoop, calls=%fused_computation.29 | loop fusion | flops 1572864 | bytes 1966080 | tf_op jit(solution)/shard_map/convert_element_type | solution.py:764
  158.4 6.4 %collective-permute-done.21 = bf16[2,4,96,512]{3,2,1,0:T(8,128)(2,1)} collective-permute-done((bf16[2,4,96,512]{3,2,1,0:T(8,128)(2,1)S(1)}, bf16[2,4,96,512]{3,2,1,0:T(8,128)(2,1)}, u32[]{:S(2)}, u32[]{:S(2)}) %collective-permute-start.21) | collective-permute-done | bytes 786464 | tf_op jit(solution)/shard_map/ppermute | solution.py:757
  164.8 2.1 fusion.3
  168.3 2.0 fusion.1
  170.9 3.6 %collective-permute-done.20.refs_2_ = bf16[192,512]{1,0:T(8,128)(2,1)} collective-permute-done((bf16[192,512]{1,0:T(8,128)(2,1)S(1)}, bf16[192,512]{1,0:T(8,128)(2,1)}, u32[]{:S(2)}, u32[]{:S(2)}) %collective-permute-start.20) | collective-permute-done | bytes 196640 | tf_op jit(solution)/shard_map/ppermute | solution.py:757
  175.1 2.3 %collective-permute-done.22 = bf16[4,96,512]{2,1,0:T(8,128)(2,1)} collective-permute-done((bf16[4,96,512]{2,1,0:T(8,128)(2,1)}, bf16[4,96,512]{2,1,0:T(8,128)(2,1)}, u32[]{:S(2)}, u32[]{:S(2)}) %collective-permute-start.22) | collective-permute-done | bytes 393248 | tf_op jit(solution)/shard_map/ppermute | solution.py:757
  177.4 1.7 fusion.19
  180.3 1.8 fusion.27
  187.7 1.5 collective-permute-start.30
  190.9 5.8 %collective-permute-done.24 = bf16[192,512]{1,0:T(8,128)(2,1)S(1)} collective-permute-done((bf16[192,512]{1,0:T(8,128)(2,1)S(1)}, bf16[192,512]{1,0:T(8,128)(2,1)S(1)}, u32[]{:S(2)}, u32[]{:S(2)}) %collective-permute-start.24) | collective-permute-done | bytes 196640 | tf_op jit(solution)/shard_map/ppermute | solution.py:757
  196.7 4.0 %collective-permute-done.25 = bf16[192,512]{1,0:T(8,128)(2,1)S(1)} collective-permute-done((bf16[192,512]{1,0:T(8,128)(2,1)S(1)}, bf16[192,512]{1,0:T(8,128)(2,1)S(1)}, u32[]{:S(2)}, u32[]{:S(2)}) %collective-permute-start.25) | collective-permute-done | bytes 196640 | tf_op jit(solution)/shard_map/ppermute | solution.py:757
  201.8 1.5 collective-permute-start.27
  204.4 1.9 shard_map.266
  206.4 2.8 %collective-permute-done.28.p3 = bf16[192,512]{1,0:T(8,128)(2,1)S(1)} collective-permute-done((bf16[192,512]{1,0:T(8,128)(2,1)S(1)}, bf16[192,512]{1,0:T(8,128)(2,1)S(1)}, u32[]{:S(2)}, u32[]{:S(2)}) %collective-permute-start.28) | collective-permute-done | bytes 196640 | tf_op jit(solution)/shard_map/ppermute | solution.py:757
  209.2 1.7 collective-permute-done.27.p2
  210.9 1.9 shard_map.265
  (140 shorter events, 40.4 us)
Async XLA Ops:
  5.5 24.8 %collective-permute-start.1 = (bf16[2,3,32,512]{3,2,1,0:T(8,128)(2,1)S(1)}, bf16[2,3,32,512]{3,2,1,0:T(8,128)(2,1)S(1)}, u32[]{:S(2)}, u32[]{:S(2)}) collective-permute-start(bf16[2,3,32,512]{3,2,1,0:T(8,128)(2,1)S(1)} %pad_maximum_fusion), channel_id=1, source_target_pairs={{0,2},{1,3},{2,0},{3,1},{4,6},{5,7},{6,4},{7,5},{8,10},{9,11},{10,... | collective-permute-start | bytes 589832 | tf_op jit(solution)/shard_map/ppermute | solution.py:757
  7.1 23.1 %collective-permute-start.2 = (bf16[2,3,32,512]{3,2,1,0:T(8,128)(2,1)S(1)}, bf16[2,3,32,512]{3,2,1,0:T(8,128)(2,1)S(1)}, u32[]{:S(2)}, u32[]{:S(2)}) collective-permute-start(bf16[2,3,32,512]{3,2,1,0:T(8,128)(2,1)S(1)} %pad_maximum_fusion.1), channel_id=1, source_target_pairs={{0,4},{1,5},{2,6},{3,7},{4,0},{5,1},{6,2},{7,3},{8,12},{9,13},{10,... | collective-permute-start | bytes 589832 | tf_op jit(solution)/shard_map/ppermute | solution.py:757
  7.6 22.7 %collective-permute-start.3 = (bf16[2,3,32,512]{3,2,1,0:T(8,128)(2,1)S(1)}, bf16[2,3,32,512]{3,2,1,0:T(8,128)(2,1)S(1)}, u32[]{:S(2)}, u32[]{:S(2)}) collective-permute-start(bf16[2,3,32,512]{3,2,1,0:T(8,128)(2,1)S(1)} %pad_maximum_fusion.2), channel_id=1, source_target_pairs={{0,6},{1,7},{2,4},{3,5},{4,2},{5,3},{6,0},{7,1},{8,14},{9,15},{10,... | collective-permute-start | bytes 589832 | tf_op jit(solution)/shard_map/ppermute | solution.py:757
  24.0 27.1 %all-to-all-start = ((bf16[8,3,32,512]{3,2,1,0:T(8,128)(2,1)}), bf16[8,3,32,512]{3,2,1,0:T(8,128)(2,1)}, u32[]{:S(2)}, u32[]{:S(2)}) async-start(bf16[8,3,32,512]{3,2,1,0:T(8,128)(2,1)} %get-tuple-element.93.refs_15_), calls=%async_computation | async-start | bytes 1572864 | tf_op jit(solution)/shard_map/all_to_all | solution.py:927
  76.5 17.4 %collective-permute-start.7 = (bf16[2,3,32,512]{3,2,1,0:T(8,128)(2,1)S(1)}, bf16[2,3,32,512]{3,2,1,0:T(8,128)(2,1)S(1)}, u32[]{:S(2)}, u32[]{:S(2)}) collective-permute-start(bf16[2,3,32,512]{3,2,1,0:T(8,128)(2,1)S(1)} %pad_maximum_fusion.3), channel_id=1, source_target_pairs={{0,2},{1,3},{2,0},{3,1},{4,6},{5,7},{6,4},{7,5},{8,10},{9,11},{10,... | collective-permute-start | bytes 589832 | tf_op jit(solution)/shard_map/ppermute | solution.py:757
  78.0 15.9 %collective-permute-start.8 = (bf16[2,3,32,512]{3,2,1,0:T(8,128)(2,1)S(1)}, bf16[2,3,32,512]{3,2,1,0:T(8,128)(2,1)S(1)}, u32[]{:S(2)}, u32[]{:S(2)}) collective-permute-start(bf16[2,3,32,512]{3,2,1,0:T(8,128)(2,1)S(1)} %pad_maximum_fusion.4), channel_id=1, source_target_pairs={{0,4},{1,5},{2,6},{3,7},{4,0},{5,1},{6,2},{7,3},{8,12},{9,13},{10,... | collective-permute-start | bytes 589832 | tf_op jit(solution)/shard_map/ppermute | solution.py:757
  78.7 18.8 %collective-permute-start.9 = (bf16[2,3,32,512]{3,2,1,0:T(8,128)(2,1)S(1)}, bf16[2,3,32,512]{3,2,1,0:T(8,128)(2,1)S(1)}, u32[]{:S(2)}, u32[]{:S(2)}) collective-permute-start(bf16[2,3,32,512]{3,2,1,0:T(8,128)(2,1)S(1)} %pad_maximum_fusion.5), channel_id=1, source_target_pairs={{0,6},{1,7},{2,4},{3,5},{4,2},{5,3},{6,0},{7,1},{8,14},{9,15},{10,... | collective-permute-start | bytes 589832 | tf_op jit(solution)/shard_map/ppermute | solution.py:757
  93.3 9.8 %collective-permute-start.4 = (bf16[4,4,96,512]{3,2,1,0:T(8,128)(2,1)}, bf16[4,4,96,512]{3,2,1,0:T(8,128)(2,1)}, u32[]{:S(2)}, u32[]{:S(2)}) collective-permute-start(bf16[4,4,96,512]{3,2,1,0:T(8,128)(2,1)} %get-tuple-element.111), channel_id=1, source_target_pairs={{0,1},{1,0},{2,3},{3,2},{4,5},{5,4},{6,7},{7,6},{8,9},{9,8},{10,11... | collective-permute-start | bytes 4718600 | tf_op jit(solution)/shard_map/ppermute | solution.py:757
  93.4 9.7 %collective-permute-start.5 = (bf16[4,4,96,512]{3,2,1,0:T(8,128)(2,1)}, bf16[4,4,96,512]{3,2,1,0:T(8,128)(2,1)}, u32[]{:S(2)}, u32[]{:S(2)}) collective-permute-start(bf16[4,4,96,512]{3,2,1,0:T(8,128)(2,1)} %get-tuple-element.112), channel_id=1, source_target_pairs={{0,1},{1,0},{2,3},{3,2},{4,5},{5,4},{6,7},{7,6},{8,9},{9,8},{10,11... | collective-permute-start | bytes 4718600 | tf_op jit(solution)/shard_map/ppermute | solution.py:757
  98.1 44.6 %all-to-all-start.1 = ((bf16[8,3,32,512]{3,2,1,0:T(8,128)(2,1)}), bf16[8,3,32,512]{3,2,1,0:T(8,128)(2,1)}, u32[]{:S(2)}, u32[]{:S(2)}) async-start(bf16[8,3,32,512]{3,2,1,0:T(8,128)(2,1)} %get-tuple-element.142), calls=%async_computation.1 | async-start | bytes 1572864 | tf_op jit(solution)/shard_map/all_to_all | solution.py:927
  107.4 24.8 %collective-permute-start.11 = (bf16[2,4,96,512]{3,2,1,0:T(8,128)(2,1)}, bf16[2,4,96,512]{3,2,1,0:T(8,128)(2,1)S(1)}, u32[]{:S(2)}, u32[]{:S(2)}) collective-permute-start(bf16[2,4,96,512]{3,2,1,0:T(8,128)(2,1)} %get-tuple-element.198.refs_27_), channel_id=1, source_target_pairs={{0,16},{8,24},{16,0},{24,8},{1,17},{9,25},{17,1},{25,9},{2,18},{10... | collective-permute-start | bytes 2359304 | tf_op jit(solution)/shard_map/ppermute | solution.py:757
  108.9 26.6 %collective-permute-start.13 = (bf16[2,4,96,512]{3,2,1,0:T(8,128)(2,1)}, bf16[2,4,96,512]{3,2,1,0:T(8,128)(2,1)}, u32[]{:S(2)}, u32[]{:S(2)}) collective-permute-start(bf16[2,4,96,512]{3,2,1,0:T(8,128)(2,1)} %get-tuple-element.199.refs_26_), channel_id=1, source_target_pairs={{0,8},{8,0},{16,24},{24,16},{1,9},{9,1},{17,25},{25,17},{2,10},{10... | collective-permute-start | bytes 2359304 | tf_op jit(solution)/shard_map/ppermute | solution.py:757
  131.6 5.8 %collective-permute-start.10 = (bf16[4,4,96,512]{3,2,1,0:T(8,128)(2,1)}, bf16[4,4,96,512]{3,2,1,0:T(8,128)(2,1)}, u32[]{:S(2)}, u32[]{:S(2)}) collective-permute-start(bf16[4,4,96,512]{3,2,1,0:T(8,128)(2,1)} %get-tuple-element.146), channel_id=1, source_target_pairs={{0,1},{1,0},{2,3},{3,2},{4,5},{5,4},{6,7},{7,6},{8,9},{9,8},{10,11... | collective-permute-start | bytes 4718600 | tf_op jit(solution)/shard_map/ppermute | solution.py:757
  131.7 6.0 %collective-permute-start.12 = (bf16[4,4,96,512]{3,2,1,0:T(8,128)(2,1)}, bf16[4,4,96,512]{3,2,1,0:T(8,128)(2,1)}, u32[]{:S(2)}, u32[]{:S(2)}) collective-permute-start(bf16[4,4,96,512]{3,2,1,0:T(8,128)(2,1)} %get-tuple-element.149), channel_id=1, source_target_pairs={{0,1},{1,0},{2,3},{3,2},{4,5},{5,4},{6,7},{7,6},{8,9},{9,8},{10,11... | collective-permute-start | bytes 4718600 | tf_op jit(solution)/shard_map/ppermute | solution.py:757
  134.9 15.1 %collective-permute-start.17 = (bf16[4,96,512]{2,1,0:T(8,128)(2,1)}, bf16[4,96,512]{2,1,0:T(8,128)(2,1)}, u32[]{:S(2)}, u32[]{:S(2)}) collective-permute-start(bf16[4,96,512]{2,1,0:T(8,128)(2,1)} %fusion.refs_0_), channel_id=1, source_target_pairs={{0,8},{8,0},{16,24},{24,16},{1,9},{9,1},{17,25},{25,17},{2,10},{10... | collective-permute-start | bytes 1179656 | tf_op jit(solution)/shard_map/ppermute | solution.py:757
  136.9 15.5 %collective-permute-start.16 = (bf16[4,96,512]{2,1,0:T(8,128)(2,1)S(1)}, bf16[4,96,512]{2,1,0:T(8,128)(2,1)}, u32[]{:S(2)}, u32[]{:S(2)}) collective-permute-start(bf16[4,96,512]{2,1,0:T(8,128)(2,1)S(1)} %fusion.2), channel_id=1, source_target_pairs={{0,16},{8,24},{16,0},{24,8},{1,17},{9,25},{17,1},{25,9},{2,18},{10... | collective-permute-start | bytes 1179656 | tf_op jit(solution)/shard_map/ppermute | solution.py:757
  139.8 25.0 %collective-permute-start.21 = (bf16[2,4,96,512]{3,2,1,0:T(8,128)(2,1)S(1)}, bf16[2,4,96,512]{3,2,1,0:T(8,128)(2,1)}, u32[]{:S(2)}, u32[]{:S(2)}) collective-permute-start(bf16[2,4,96,512]{3,2,1,0:T(8,128)(2,1)S(1)} %get-tuple-element.196.refs_11_), channel_id=1, source_target_pairs={{0,16},{8,24},{16,0},{24,8},{1,17},{9,25},{17,1},{25,9},{2,18},{10... | collective-permute-start | bytes 2359304 | tf_op jit(solution)/shard_map/ppermute | solution.py:757
  141.2 27.1 %collective-permute-start.14 = (bf16[2,4,96,512]{3,2,1,0:T(8,128)(2,1)S(1)}, bf16[2,4,96,512]{3,2,1,0:T(8,128)(2,1)}, u32[]{:S(2)}, u32[]{:S(2)}) collective-permute-start(bf16[2,4,96,512]{3,2,1,0:T(8,128)(2,1)S(1)} %get-tuple-element.197.refs_10_), channel_id=1, source_target_pairs={{0,8},{8,0},{16,24},{24,16},{1,9},{9,1},{17,25},{25,17},{2,10},{10... | collective-permute-start | bytes 2359304 | tf_op jit(solution)/shard_map/ppermute | solution.py:757
  154.7 16.2 %collective-permute-start.18 = (bf16[192,512]{1,0:T(8,128)(2,1)S(1)}, bf16[192,512]{1,0:T(8,128)(2,1)S(1)}, u32[]{:S(2)}, u32[]{:S(2)}) collective-permute-start(bf16[192,512]{1,0:T(8,128)(2,1)S(1)} %pad_maximum_fusion.6), channel_id=1, source_target_pairs={{0,2},{1,3},{2,0},{3,1},{4,6},{5,7},{6,4},{7,5},{8,10},{9,11},{10,... | collective-permute-start | bytes 589832 | tf_op jit(solution)/shard_map/ppermute | solution.py:757
  156.2 14.6 %collective-permute-start.19 = (bf16[192,512]{1,0:T(8,128)(2,1)S(1)}, bf16[192,512]{1,0:T(8,128)(2,1)S(1)}, u32[]{:S(2)}, u32[]{:S(2)}) collective-permute-start(bf16[192,512]{1,0:T(8,128)(2,1)S(1)} %pad_maximum_fusion.7), channel_id=1, source_target_pairs={{0,4},{1,5},{2,6},{3,7},{4,0},{5,1},{6,2},{7,3},{8,12},{9,13},{10,... | collective-permute-start | bytes 589832 | tf_op jit(solution)/shard_map/ppermute | solution.py:757
  156.9 17.6 %collective-permute-start.20 = (bf16[192,512]{1,0:T(8,128)(2,1)S(1)}, bf16[192,512]{1,0:T(8,128)(2,1)}, u32[]{:S(2)}, u32[]{:S(2)}) collective-permute-start(bf16[192,512]{1,0:T(8,128)(2,1)S(1)} %pad_maximum_fusion.8), channel_id=1, source_target_pairs={{0,6},{1,7},{2,4},{3,5},{4,2},{5,3},{6,0},{7,1},{8,14},{9,15},{10,... | collective-permute-start | bytes 589832 | tf_op jit(solution)/shard_map/ppermute | solution.py:757
  167.0 10.4 %collective-permute-start.22 = (bf16[4,96,512]{2,1,0:T(8,128)(2,1)}, bf16[4,96,512]{2,1,0:T(8,128)(2,1)}, u32[]{:S(2)}, u32[]{:S(2)}) collective-permute-start(bf16[4,96,512]{2,1,0:T(8,128)(2,1)} %fusion.3), channel_id=1, source_target_pairs={{0,8},{8,0},{16,24},{24,16},{1,9},{9,1},{17,25},{25,17},{2,10},{10... | collective-permute-start | bytes 1179656 | tf_op jit(solution)/shard_map/ppermute | solution.py:757
  170.3 10.0 %collective-permute-start.15 = (bf16[4,96,512]{2,1,0:T(8,128)(2,1)}, bf16[4,96,512]{2,1,0:T(8,128)(2,1)}, u32[]{:S(2)}, u32[]{:S(2)}) collective-permute-start(bf16[4,96,512]{2,1,0:T(8,128)(2,1)} %fusion.1), channel_id=1, source_target_pairs={{0,16},{8,24},{16,0},{24,8},{1,17},{9,25},{17,1},{25,9},{2,18},{10... | collective-permute-start | bytes 1179656 | tf_op jit(solution)/shard_map/ppermute | solution.py:757
  182.2 8.0 %collective-permute-start.23 = (bf16[192,512]{1,0:T(8,128)(2,1)S(1)}, bf16[192,512]{1,0:T(8,128)(2,1)S(1)}, u32[]{:S(2)}, u32[]{:S(2)}) collective-permute-start(bf16[192,512]{1,0:T(8,128)(2,1)S(1)} %pad_maximum_fusion.9), channel_id=1, source_target_pairs={{0,2},{1,3},{2,0},{3,1},{4,6},{5,7},{6,4},{7,5},{8,10},{9,11},{10,... | collective-permute-start | bytes 589832 | tf_op jit(solution)/shard_map/ppermute | solution.py:757
  183.7 13.0 %collective-permute-start.24 = (bf16[192,512]{1,0:T(8,128)(2,1)S(1)}, bf16[192,512]{1,0:T(8,128)(2,1)S(1)}, u32[]{:S(2)}, u32[]{:S(2)}) collective-permute-start(bf16[192,512]{1,0:T(8,128)(2,1)S(1)} %pad_maximum_fusion.10), channel_id=1, source_target_pairs={{0,4},{1,5},{2,6},{3,7},{4,0},{5,1},{6,2},{7,3},{8,12},{9,13},{10,... | collective-permute-start | bytes 589832 | tf_op jit(solution)/shard_map/ppermute | solution.py:757
  184.4 16.3 %collective-permute-start.25 = (bf16[192,512]{1,0:T(8,128)(2,1)S(1)}, bf16[192,512]{1,0:T(8,128)(2,1)S(1)}, u32[]{:S(2)}, u32[]{:S(2)}) collective-permute-start(bf16[192,512]{1,0:T(8,128)(2,1)S(1)} %pad_maximum_fusion.11), channel_id=1, source_target_pairs={{0,6},{1,7},{2,4},{3,5},{4,2},{5,3},{6,0},{7,1},{8,14},{9,15},{10,... | collective-permute-start | bytes 589832 | tf_op jit(solution)/shard_map/ppermute | solution.py:757
  186.9 16.4 %collective-permute-start.31 = (bf16[192,512]{1,0:T(8,128)(2,1)S(1)}, bf16[192,512]{1,0:T(8,128)(2,1)S(1)}, u32[]{:S(2)}, u32[]{:S(2)}) collective-permute-start(bf16[192,512]{1,0:T(8,128)(2,1)S(1)} %add_convert_fusion.8.p0), channel_id=1, source_target_pairs={{0,24},{8,16},{16,8},{24,0},{1,25},{9,17},{17,9},{25,1},{2,26},{10... | collective-permute-start | bytes 589832 | tf_op jit(solution)/shard_map/ppermute | solution.py:757
  187.7 16.6 %collective-permute-start.30 = (bf16[192,512]{1,0:T(8,128)(2,1)S(1)}, bf16[192,512]{1,0:T(8,128)(2,1)S(1)}, u32[]{:S(2)}, u32[]{:S(2)}) collective-permute-start(bf16[192,512]{1,0:T(8,128)(2,1)S(1)} %add_convert_fusion.8.p0), channel_id=1, source_target_pairs={{0,16},{8,24},{16,0},{24,8},{1,17},{9,25},{17,1},{25,9},{2,18},{10... | collective-permute-start | bytes 589832 | tf_op jit(solution)/shard_map/ppermute | solution.py:757
  190.2 14.2 %collective-permute-start.29 = (bf16[192,512]{1,0:T(8,128)(2,1)S(1)}, bf16[192,512]{1,0:T(8,128)(2,1)S(1)}, u32[]{:S(2)}, u32[]{:S(2)}) collective-permute-start(bf16[192,512]{1,0:T(8,128)(2,1)S(1)} %add_convert_fusion.8.p0), channel_id=1, source_target_pairs={{0,8},{8,0},{16,24},{24,16},{1,9},{9,1},{17,25},{25,17},{2,10},{10... | collective-permute-start | bytes 589832 | tf_op jit(solution)/shard_map/ppermute | solution.py:757
  200.8 8.4 %collective-permute-start.28 = (bf16[192,512]{1,0:T(8,128)(2,1)S(1)}, bf16[192,512]{1,0:T(8,128)(2,1)S(1)}, u32[]{:S(2)}, u32[]{:S(2)}) collective-permute-start(bf16[192,512]{1,0:T(8,128)(2,1)S(1)} %add_convert_fusion.9.p0), channel_id=1, source_target_pairs={{0,24},{8,16},{16,8},{24,0},{1,25},{9,17},{17,9},{25,1},{2,26},{10... | collective-permute-start | bytes 589832 | tf_op jit(solution)/shard_map/ppermute | solution.py:757
  201.8 9.1 %collective-permute-start.27 = (bf16[192,512]{1,0:T(8,128)(2,1)S(1)}, bf16[192,512]{1,0:T(8,128)(2,1)S(1)}, u32[]{:S(2)}, u32[]{:S(2)}) collective-permute-start(bf16[192,512]{1,0:T(8,128)(2,1)S(1)} %add_convert_fusion.9.p0), channel_id=1, source_target_pairs={{0,16},{8,24},{16,0},{24,8},{1,17},{9,25},{17,1},{25,9},{2,18},{10... | collective-permute-start | bytes 589832 | tf_op jit(solution)/shard_map/ppermute | solution.py:757
  203.3 7.6 %collective-permute-start.26 = (bf16[192,512]{1,0:T(8,128)(2,1)S(1)}, bf16[192,512]{1,0:T(8,128)(2,1)S(1)}, u32[]{:S(2)}, u32[]{:S(2)}) collective-permute-start(bf16[192,512]{1,0:T(8,128)(2,1)S(1)} %add_convert_fusion.9.p0), channel_id=1, source_target_pairs={{0,8},{8,0},{16,24},{24,16},{1,9},{9,1},{17,25},{25,17},{2,10},{10... | collective-permute-start | bytes 589832 | tf_op jit(solution)/shard_map/ppermute | solution.py:757
  (33 other events, 239.0 us)
where the time goes:
time: 217 us; the launch traced here: 213 us
  Pallas kernels  107 us (49%)
  starting transfers between devices  42.1 us (19%)
  waiting for transfers between devices  34.3 us (16%)
  other arithmetic  22.8 us (11%)
  local copies, waits for them, and re-layouts  5.52 us (3%)
    pallas_call x4, Pallas kernels, manual_call(): pl.pallas_call(without(kernel, len(scalars) + len(args), len(after)), out...  72.3 us
    ppermute x32, waiting for transfers between devices, swap(): return lax.ppermute(array, axis, [(i, i ^ mask) for i in range(size)])  34.3 us
    ppermute x32, starting transfers between devices, swap(): return lax.ppermute(array, axis, [(i, i ^ mask) for i in range(size)])  31.5 us
    pallas_call x2, Pallas kernels, call(): pl.pallas_call(without(kernel, len(scalars) + len(args), unread), out_sha...  26.2 us
    convert_element_type x12, other arithmetic, add(): return total.astype(BF)  22 us
    all_to_all x2, starting transfers between devices, exchange(): return lax.all_to_all(array, 'tm', split_axis=0, concat_axis=0, tiled=True)  10.6 us
  transfers between devices with their start and end apart: 34, of which 13 were waited for; matrix products, arithmetic and copies ran while one was open for 10% of the time, Pallas kernels for 37%

commit v1 on v0

--- a/solution.py
+++ b/solution.py
@@ -274,6 +274,10 @@
         semaphore = semaphores.at[base + index * packs + pack]
         return pltpu.make_async_copy(state[index].at[pack], outs[1 + index].at[pack], semaphore)
 
+    def sending(pack):
+        part, semaphore = (slice(None), pl.ds(pack, 1)), semaphores.at[base + len(state) * packs + pack]
+        return pltpu.make_async_copy(x2.at[part], outs[0].at[part], semaphore)
+
     def first(pack, arrivals):
         pl.when(pack == 0)(lambda: wait(*arrivals))
 
@@ -291,16 +295,15 @@
             sent,
         )
         block_of(whole(steps), x2.at[:, pl.ds(pack, 1)])
+        sending(pack).start()
         return carry
 
     wait(*got)
     lax.fori_loop(0, packs, run, 0)
-    copies.count = base + len(state) * packs
-    copies.send(x2, outs[0])
-    for index in range(len(state)):
-        for pack in range(packs):
+    for pack in range(packs):
+        sending(pack).wait()
+        for index in range(len(state)):
             leaving(index, pack).wait()
-    copies.finish()
 
 
 def build_bias(labels, pack, slots, patches, bias):
@@ -980,7 +983,7 @@
         + [(w.shape, BF) for w in (space_input, space_output, space_up, space_down)]
         + space_outs
         + [((4, tokens, tokens), F32), ((2, tokens, CHUNK), BF)],
-        5 + 10 * some,
+        5 + 11 * some,
         small=2,
         after=sent,
         flops=some * flops,

time: 217 us -> 217 us (level)
  no operation moved by 1% of the time
where the time goes in v1:
time: 217 us; the launch traced here: 213 us
  Pallas kernels  107 us (49%)
  starting transfers between devices  42.1 us (19%)
  waiting for transfers between devices  34.3 us (16%)
  other arithmetic  22.8 us (11%)
  local copies, waits for them, and re-layouts  5.52 us (3%)
    pallas_call x4, Pallas kernels, manual_call(): pl.pallas_call(without(kernel, len(scalars) + len(args), len(after)), out...  72.2 us
    ppermute x32, waiting for transfers between devices, swap(): return lax.ppermute(array, axis, [(i, i ^ mask) for i in range(size)])  34.3 us
    ppermute x32, starting transfers between devices, swap(): return lax.ppermute(array, axis, [(i, i ^ mask) for i in range(size)])  31.5 us
    pallas_call x2, Pallas kernels, call(): pl.pallas_call(without(kernel, len(scalars) + len(args), unread), out_sha...  26.2 us
    convert_element_type x12, other arithmetic, add(): return total.astype(BF)  22 us
    all_to_all x2, starting transfers between devices, exchange(): return lax.all_to_all(array, 'tm', split_axis=0, concat_axis=0, tiled=True)  10.6 us
  transfers between devices with their start and end apart: 34, of which 13 were waited for; matrix products, arithmetic and copies ran while one was open for 10% of the time, Pallas kernels for 37%

profile of v1, /device:TPU:16, one launch (start us, length us, event | category | flops | bytes accessed | tf_op | source)
XLA Modules:
  0.0 213.0 jit_solution(15995593395937187987)
XLA Ops:
  1.3 2.2 %shard_map.254 = (bf16[4,3,32,512]{3,2,1,0:T(8,128)(2,1)}, bf16[4,3,32,512]{3,2,1,0:T(8,128)(2,1)}) custom-call(s32[4,8]{1,0:T(4,128)} %refs_0_.7, s32[3]{0:T(128)} %pad_add_fusion.ids.refs_1_.refs_0_, bf16[4,1,256,512]{3,2,1,0:T(8,128)(2,1)} %refs_2_.2), custom_call_target="tpu_custom_call" | custom-call | tf_op jit(solution)/shard_map/pallas_call | solution.py:886
  5.5 1.6 collective-permute-start.1
  7.6 1.6 collective-permute-start.3
  9.2 14.6 %shard_map.255 = (bf16[8,3,32,512]{3,2,1,0:T(8,128)(2,1)}, bf16[3,256,512]{2,1,0:T(8,128)(2,1)}, f32[3,256,128]{2,1,0:T(8,128)}, bf16[3,256,1536]{2,1,0:T(8,128)...) custom-call(s32[4,8]{1,0:T(4,128)} %refs_0_.7, ...), custom_call_target="tpu_custom_call" | custom-call | flops 4831838208 | tf_op jit(solution)/shard_map/pallas_call | solution.py:743
  23.8 6.3 %all-to-all-start = ((bf16[8,3,32,512]{3,2,1,0:T(8,128)(2,1)}), bf16[8,3,32,512]{3,2,1,0:T(8,128)(2,1)}, u32[]{:S(2)}, u32[]{:S(2)}) async-start(bf16[8,3,32,512]{3,2,1,0:T(8,128)(2,1)} %get-tuple-element.93.refs_15_), calls=%async_computation | async-start | bytes 1572864 | tf_op jit(solution)/shard_map/all_to_all | solution.py:930
  32.1 18.8 %shard_map.257 = (f32[4,1,256,512]{3,2,1,0:T(8,128)}, f32[4,1,256,512]{3,2,1,0:T(8,128)}, bf16[1,256,512]{2,1,0:T(8,128)(2,1)}, bf16[1,256,512]{2,1,0:T(8,128)(2...) custom-call(s32[4,8]{1,0:T(4,128)} %refs_0_.7, ...), custom_call_target="tpu_custom_call" | custom-call | flops 9663676416 | bytes 15476736 | tf_op jit(solution)/shard_map/pallas_call | solution.py:636
  51.0 23.3 %shard_map.258 = (bf16[4,3,32,512]{3,2,1,0:T(8,128)(2,1)}, bf16[4,3,32,512]{3,2,1,0:T(8,128)(2,1)}, bf16[8,3,32,512]{3,2,1,0:T(8,128)(2,1)}, bf16[3,256,512]{2,1...) custom-call(s32[4,8]{1,0:T(4,128)} %refs_0_.7, ...), custom_call_target="tpu_custom_call" | custom-call | flops 14495514624 | tf_op jit(solution)/shard_map/pallas_call | solution.py:743
  80.1 13.1 %shard_map.259 = (bf16[4,4,96,512]{3,2,1,0:T(8,128)(2,1)}, bf16[4,4,96,512]{3,2,1,0:T(8,128)(2,1)}, bf16[4,4,96,512]{3,2,1,0:T(8,128)(2,1)}, bf16[4,4,96,512]{3,2,1,0:T(8,128)(2,1)}) custom-call(s32[3]{0:T(128)} %pad_add_fusion.ids.refs_1_.refs_0_, bf16[3,256,512]{2,1,0:T(8,128)(2,1)} %get-tuple-element.95.refs_1_, ...), custom_call_target="tpu_custom_call" | custom-call | flops 6442450944 | tf_op jit(solution)/shard_map/pallas_call | solution.py:743
  93.8 3.5 %collective-permute-done.9.refs_2_.refs_7_ = bf16[2,3,32,512]{3,2,1,0:T(8,128)(2,1)S(1)} collective-permute-done((bf16[2,3,32,512]{3,2,1,0:T(8,128)(2,1)S(1)}, bf16[2,3,32,512]{3,2,1,0:T(8,128)(2,1)S(1)}, u32[]{:S(2)}, u32[]{:S(2)}) %collective-permute-start.9) | collective-permute-done | bytes 196640 | tf_op jit(solution)/shard_map/ppermute | solution.py:760
  98.0 4.3 %all-to-all-start.1 = ((bf16[8,3,32,512]{3,2,1,0:T(8,128)(2,1)}), bf16[8,3,32,512]{3,2,1,0:T(8,128)(2,1)}, u32[]{:S(2)}, u32[]{:S(2)}) async-start(bf16[8,3,32,512]{3,2,1,0:T(8,128)(2,1)} %get-tuple-element.142), calls=%async_computation.1 | async-start | bytes 1572864 | tf_op jit(solution)/shard_map/all_to_all | solution.py:930
  104.2 3.0 %add_convert_fusion.2 = (bf16[2,4,96,512]{3,2,1,0:T(8,128)(2,1)}, bf16[2,4,96,512]{3,2,1,0:T(8,128)(2,1)}) fusion(bf16[4,4,96,512]{3,2,1,0:T(8,128)(2,1)} %collective-permute-done.5, bf16[4,4,96,512]{3,2,1,0:T(8,128)(2,1)S(1)} %copy-done.13, f32[512]{0:T(512)} %bitcast.151, bf16[4,4,96,512]{3,2,1,0:T(8,128)(2,1)} %collective-permute-done.4, ...), kind=kLoop, calls=%fused_computation.2 | loop fusion | flops 3932160 | bytes 4720640 | tf_op jit(solution)/shard_map/convert_element_type | solution.py:767
  110.3 21.2 %shard_map.261 = (f32[3,256,512]{2,1,0:T(8,128)}, bf16[3,256,1536]{2,1,0:T(8,128)(2,1)}, bf16[4,4,96,512]{3,2,1,0:T(8,128)(2,1)}, bf16[4,4,96,512]{3,2,1,0:T(8,1...) custom-call(s32[3]{0:T(128)} %pad_add_fusion.ids.refs_1_.refs_0_, f32[1,512]{1,0:T(1,128)} %bitcast.146, ...), custom_call_target="tpu_custom_call" | custom-call | flops 12884901888 | tf_op jit(solution)/shard_map/pallas_call | solution.py:743
  132.1 2.2 %fusion.refs_0_ = bf16[4,96,512]{2,1,0:T(8,128)(2,1)} fusion(bf16[2,4,96,512]{3,2,1,0:T(8,128)(2,1)S(1)} %collective-permute-done.11, bf16[4,4,96,512]{3,2,1,0:T(8,128)(2,1)} %collective-permute-done.5, bf16[4,4,96,512]{3,2,1,0:T(8,128)(2,1)S(1)} %copy-done.13), kind=kLoop, calls=%fused_computation.8 | loop fusion | flops 1179648 | bytes 1572864 | tf_op jit(solution)/shard_map/convert_element_type | solution.py:767
  137.6 2.1 add_convert_fusion
  142.6 7.4 %shard_map.263 = (f32[4,1,256,512]{3,2,1,0:T(8,128)}, f32[4,1,256,512]{3,2,1,0:T(8,128)}) custom-call(s32[4,8]{1,0:T(4,128)} %refs_0_.7, bf16[3,256,1536]{2,1,0:T(8,128)(2,1)} %get-tuple-element.139.refs_1_, bf16[512,1536]{1,0:T(8,128)(2,1)} %w_in.2, f32[1,512]{1,0:T(1,128)} %bitcast.136, ...), custom_call_target="tpu_custom_call", output_to_operand_aliasing={{0}: (8, {}), {1}: (9, {})} | custom-call | flops 1207959552 | bytes 13240320 | tf_op jit(solution)/shard_map/pallas_call | solution.py:636
  149.9 2.3 %fusion.4 = (bf16[96,512]{1,0:T(8,128)(2,1)}, bf16[96,512]{1,0:T(8,128)(2,1)S(1)}, bf16[96,512]{1,0:T(8,128)(2,1)S(1)}, bf16[96,512]{1,0:T(8,128)(2,1)S(1)}) fusion(bf16[4,96,512]{2,1,0:T(8,128)(2,1)} %collective-permute-done.17, bf16[2,4,96,512]{3,2,1,0:T(8,128)(2,1)} %copy-done.14, bf16[4,4,96,512]{3,2,1,0:T(8,128)(2,1)} %collective-permute-done.5, ...), kind=kLoop, calls=%fused_computation.27 | loop fusion | flops 1572864 | bytes 1966080 | tf_op jit(solution)/shard_map/convert_element_type | solution.py:767
  152.2 2.3 %fusion.5 = (bf16[96,512]{1,0:T(8,128)(2,1)}, bf16[96,512]{1,0:T(8,128)(2,1)S(1)}, bf16[96,512]{1,0:T(8,128)(2,1)S(1)}, bf16[96,512]{1,0:T(8,128)(2,1)S(1)}) fusion(bf16[4,96,512]{2,1,0:T(8,128)(2,1)} %collective-permute-done.16, bf16[2,4,96,512]{3,2,1,0:T(8,128)(2,1)} %collective-permute-done.13, bf16[4,4,96,512]{3,2,1,0:T(8,128)(2,1)} %collective-permute-done.4, ...), kind=kLoop, calls=%fused_computation.29 | loop fusion | flops 1572864 | bytes 1966080 | tf_op jit(solution)/shard_map/convert_element_type | solution.py:767
  154.6 1.5 collective-permute-start.18
  158.3 6.4 %collective-permute-done.21 = bf16[2,4,96,512]{3,2,1,0:T(8,128)(2,1)} collective-permute-done((bf16[2,4,96,512]{3,2,1,0:T(8,128)(2,1)S(1)}, bf16[2,4,96,512]{3,2,1,0:T(8,128)(2,1)}, u32[]{:S(2)}, u32[]{:S(2)}) %collective-permute-start.21) | collective-permute-done | bytes 786464 | tf_op jit(solution)/shard_map/ppermute | solution.py:760
  164.7 2.1 fusion.3
  168.2 2.0 fusion.1
  170.8 3.6 %collective-permute-done.20.refs_2_ = bf16[192,512]{1,0:T(8,128)(2,1)} collective-permute-done((bf16[192,512]{1,0:T(8,128)(2,1)S(1)}, bf16[192,512]{1,0:T(8,128)(2,1)}, u32[]{:S(2)}, u32[]{:S(2)}) %collective-permute-start.20) | collective-permute-done | bytes 196640 | tf_op jit(solution)/shard_map/ppermute | solution.py:760
  175.0 2.2 %collective-permute-done.22 = bf16[4,96,512]{2,1,0:T(8,128)(2,1)} collective-permute-done((bf16[4,96,512]{2,1,0:T(8,128)(2,1)}, bf16[4,96,512]{2,1,0:T(8,128)(2,1)}, u32[]{:S(2)}, u32[]{:S(2)}) %collective-permute-start.22) | collective-permute-done | bytes 393248 | tf_op jit(solution)/shard_map/ppermute | solution.py:760
  177.2 1.7 fusion.19
  180.2 1.8 fusion.27
  190.8 5.8 %collective-permute-done.24 = bf16[192,512]{1,0:T(8,128)(2,1)S(1)} collective-permute-done((bf16[192,512]{1,0:T(8,128)(2,1)S(1)}, bf16[192,512]{1,0:T(8,128)(2,1)S(1)}, u32[]{:S(2)}, u32[]{:S(2)}) %collective-permute-start.24) | collective-permute-done | bytes 196640 | tf_op jit(solution)/shard_map/ppermute | solution.py:760
  196.6 4.0 %collective-permute-done.25 = bf16[192,512]{1,0:T(8,128)(2,1)S(1)} collective-permute-done((bf16[192,512]{1,0:T(8,128)(2,1)S(1)}, bf16[192,512]{1,0:T(8,128)(2,1)S(1)}, u32[]{:S(2)}, u32[]{:S(2)}) %collective-permute-start.25) | collective-permute-done | bytes 196640 | tf_op jit(solution)/shard_map/ppermute | solution.py:760
  201.7 1.5 collective-permute-start.27
  204.3 1.9 shard_map.266
  206.3 2.8 %collective-permute-done.28.p3 = bf16[192,512]{1,0:T(8,128)(2,1)S(1)} collective-permute-done((bf16[192,512]{1,0:T(8,128)(2,1)S(1)}, bf16[192,512]{1,0:T(8,128)(2,1)S(1)}, u32[]{:S(2)}, u32[]{:S(2)}) %collective-permute-start.28) | collective-permute-done | bytes 196640 | tf_op jit(solution)/shard_map/ppermute | solution.py:760
  209.1 1.7 collective-permute-done.27.p2
  210.8 1.9 shard_map.265
  (140 shorter events, 40.5 us)
Async XLA Ops:
  5.5 24.7 %collective-permute-start.1 = (bf16[2,3,32,512]{3,2,1,0:T(8,128)(2,1)S(1)}, bf16[2,3,32,512]{3,2,1,0:T(8,128)(2,1)S(1)}, u32[]{:S(2)}, u32[]{:S(2)}) collective-permute-start(bf16[2,3,32,512]{3,2,1,0:T(8,128)(2,1)S(1)} %pad_maximum_fusion), channel_id=1, source_target_pairs={{0,2},{1,3},{2,0},{3,1},{4,6},{5,7},{6,4},{7,5},{8,10},{9,11},{10,... | collective-permute-start | bytes 589832 | tf_op jit(solution)/shard_map/ppermute | solution.py:760
  7.1 23.0 %collective-permute-start.2 = (bf16[2,3,32,512]{3,2,1,0:T(8,128)(2,1)S(1)}, bf16[2,3,32,512]{3,2,1,0:T(8,128)(2,1)S(1)}, u32[]{:S(2)}, u32[]{:S(2)}) collective-permute-start(bf16[2,3,32,512]{3,2,1,0:T(8,128)(2,1)S(1)} %pad_maximum_fusion.1), channel_id=1, source_target_pairs={{0,4},{1,5},{2,6},{3,7},{4,0},{5,1},{6,2},{7,3},{8,12},{9,13},{10,... | collective-permute-start | bytes 589832 | tf_op jit(solution)/shard_map/ppermute | solution.py:760
  7.6 22.6 %collective-permute-start.3 = (bf16[2,3,32,512]{3,2,1,0:T(8,128)(2,1)S(1)}, bf16[2,3,32,512]{3,2,1,0:T(8,128)(2,1)S(1)}, u32[]{:S(2)}, u32[]{:S(2)}) collective-permute-start(bf16[2,3,32,512]{3,2,1,0:T(8,128)(2,1)S(1)} %pad_maximum_fusion.2), channel_id=1, source_target_pairs={{0,6},{1,7},{2,4},{3,5},{4,2},{5,3},{6,0},{7,1},{8,14},{9,15},{10,... | collective-permute-start | bytes 589832 | tf_op jit(solution)/shard_map/ppermute | solution.py:760
  23.8 27.1 %all-to-all-start = ((bf16[8,3,32,512]{3,2,1,0:T(8,128)(2,1)}), bf16[8,3,32,512]{3,2,1,0:T(8,128)(2,1)}, u32[]{:S(2)}, u32[]{:S(2)}) async-start(bf16[8,3,32,512]{3,2,1,0:T(8,128)(2,1)} %get-tuple-element.93.refs_15_), calls=%async_computation | async-start | bytes 1572864 | tf_op jit(solution)/shard_map/all_to_all | solution.py:930
  76.3 17.4 %collective-permute-start.7 = (bf16[2,3,32,512]{3,2,1,0:T(8,128)(2,1)S(1)}, bf16[2,3,32,512]{3,2,1,0:T(8,128)(2,1)S(1)}, u32[]{:S(2)}, u32[]{:S(2)}) collective-permute-start(bf16[2,3,32,512]{3,2,1,0:T(8,128)(2,1)S(1)} %pad_maximum_fusion.3), channel_id=1, source_target_pairs={{0,2},{1,3},{2,0},{3,1},{4,6},{5,7},{6,4},{7,5},{8,10},{9,11},{10,... | collective-permute-start | bytes 589832 | tf_op jit(solution)/shard_map/ppermute | solution.py:760
  77.9 15.9 %collective-permute-start.8 = (bf16[2,3,32,512]{3,2,1,0:T(8,128)(2,1)S(1)}, bf16[2,3,32,512]{3,2,1,0:T(8,128)(2,1)S(1)}, u32[]{:S(2)}, u32[]{:S(2)}) collective-permute-start(bf16[2,3,32,512]{3,2,1,0:T(8,128)(2,1)S(1)} %pad_maximum_fusion.4), channel_id=1, source_target_pairs={{0,4},{1,5},{2,6},{3,7},{4,0},{5,1},{6,2},{7,3},{8,12},{9,13},{10,... | collective-permute-start | bytes 589832 | tf_op jit(solution)/shard_map/ppermute | solution.py:760
  78.6 18.8 %collective-permute-start.9 = (bf16[2,3,32,512]{3,2,1,0:T(8,128)(2,1)S(1)}, bf16[2,3,32,512]{3,2,1,0:T(8,128)(2,1)S(1)}, u32[]{:S(2)}, u32[]{:S(2)}) collective-permute-start(bf16[2,3,32,512]{3,2,1,0:T(8,128)(2,1)S(1)} %pad_maximum_fusion.5), channel_id=1, source_target_pairs={{0,6},{1,7},{2,4},{3,5},{4,2},{5,3},{6,0},{7,1},{8,14},{9,15},{10,... | collective-permute-start | bytes 589832 | tf_op jit(solution)/shard_map/ppermute | solution.py:760
  93.2 9.8 %collective-permute-start.4 = (bf16[4,4,96,512]{3,2,1,0:T(8,128)(2,1)}, bf16[4,4,96,512]{3,2,1,0:T(8,128)(2,1)}, u32[]{:S(2)}, u32[]{:S(2)}) collective-permute-start(bf16[4,4,96,512]{3,2,1,0:T(8,128)(2,1)} %get-tuple-element.111), channel_id=1, source_target_pairs={{0,1},{1,0},{2,3},{3,2},{4,5},{5,4},{6,7},{7,6},{8,9},{9,8},{10,11... | collective-permute-start | bytes 4718600 | tf_op jit(solution)/shard_map/ppermute | solution.py:760
  93.3 9.7 %collective-permute-start.5 = (bf16[4,4,96,512]{3,2,1,0:T(8,128)(2,1)}, bf16[4,4,96,512]{3,2,1,0:T(8,128)(2,1)}, u32[]{:S(2)}, u32[]{:S(2)}) collective-permute-start(bf16[4,4,96,512]{3,2,1,0:T(8,128)(2,1)} %get-tuple-element.112), channel_id=1, source_target_pairs={{0,1},{1,0},{2,3},{3,2},{4,5},{5,4},{6,7},{7,6},{8,9},{9,8},{10,11... | collective-permute-start | bytes 4718600 | tf_op jit(solution)/shard_map/ppermute | solution.py:760
  98.0 44.6 %all-to-all-start.1 = ((bf16[8,3,32,512]{3,2,1,0:T(8,128)(2,1)}), bf16[8,3,32,512]{3,2,1,0:T(8,128)(2,1)}, u32[]{:S(2)}, u32[]{:S(2)}) async-start(bf16[8,3,32,512]{3,2,1,0:T(8,128)(2,1)} %get-tuple-element.142), calls=%async_computation.1 | async-start | bytes 1572864 | tf_op jit(solution)/shard_map/all_to_all | solution.py:930
  107.2 24.8 %collective-permute-start.11 = (bf16[2,4,96,512]{3,2,1,0:T(8,128)(2,1)}, bf16[2,4,96,512]{3,2,1,0:T(8,128)(2,1)S(1)}, u32[]{:S(2)}, u32[]{:S(2)}) collective-permute-start(bf16[2,4,96,512]{3,2,1,0:T(8,128)(2,1)} %get-tuple-element.198.refs_27_), channel_id=1, source_target_pairs={{0,16},{8,24},{16,0},{24,8},{1,17},{9,25},{17,1},{25,9},{2,18},{10... | collective-permute-start | bytes 2359304 | tf_op jit(solution)/shard_map/ppermute | solution.py:760
  108.8 26.6 %collective-permute-start.13 = (bf16[2,4,96,512]{3,2,1,0:T(8,128)(2,1)}, bf16[2,4,96,512]{3,2,1,0:T(8,128)(2,1)}, u32[]{:S(2)}, u32[]{:S(2)}) collective-permute-start(bf16[2,4,96,512]{3,2,1,0:T(8,128)(2,1)} %get-tuple-element.199.refs_26_), channel_id=1, source_target_pairs={{0,8},{8,0},{16,24},{24,16},{1,9},{9,1},{17,25},{25,17},{2,10},{10... | collective-permute-start | bytes 2359304 | tf_op jit(solution)/shard_map/ppermute | solution.py:760
  131.5 5.8 %collective-permute-start.10 = (bf16[4,4,96,512]{3,2,1,0:T(8,128)(2,1)}, bf16[4,4,96,512]{3,2,1,0:T(8,128)(2,1)}, u32[]{:S(2)}, u32[]{:S(2)}) collective-permute-start(bf16[4,4,96,512]{3,2,1,0:T(8,128)(2,1)} %get-tuple-element.146), channel_id=1, source_target_pairs={{0,1},{1,0},{2,3},{3,2},{4,5},{5,4},{6,7},{7,6},{8,9},{9,8},{10,11... | collective-permute-start | bytes 4718600 | tf_op jit(solution)/shard_map/ppermute | solution.py:760
  131.6 6.0 %collective-permute-start.12 = (bf16[4,4,96,512]{3,2,1,0:T(8,128)(2,1)}, bf16[4,4,96,512]{3,2,1,0:T(8,128)(2,1)}, u32[]{:S(2)}, u32[]{:S(2)}) collective-permute-start(bf16[4,4,96,512]{3,2,1,0:T(8,128)(2,1)} %get-tuple-element.149), channel_id=1, source_target_pairs={{0,1},{1,0},{2,3},{3,2},{4,5},{5,4},{6,7},{7,6},{8,9},{9,8},{10,11... | collective-permute-start | bytes 4718600 | tf_op jit(solution)/shard_map/ppermute | solution.py:760
  134.8 15.1 %collective-permute-start.17 = (bf16[4,96,512]{2,1,0:T(8,128)(2,1)}, bf16[4,96,512]{2,1,0:T(8,128)(2,1)}, u32[]{:S(2)}, u32[]{:S(2)}) collective-permute-start(bf16[4,96,512]{2,1,0:T(8,128)(2,1)} %fusion.refs_0_), channel_id=1, source_target_pairs={{0,8},{8,0},{16,24},{24,16},{1,9},{9,1},{17,25},{25,17},{2,10},{10... | collective-permute-start | bytes 1179656 | tf_op jit(solution)/shard_map/ppermute | solution.py:760
  136.7 15.5 %collective-permute-start.16 = (bf16[4,96,512]{2,1,0:T(8,128)(2,1)S(1)}, bf16[4,96,512]{2,1,0:T(8,128)(2,1)}, u32[]{:S(2)}, u32[]{:S(2)}) collective-permute-start(bf16[4,96,512]{2,1,0:T(8,128)(2,1)S(1)} %fusion.2), channel_id=1, source_target_pairs={{0,16},{8,24},{16,0},{24,8},{1,17},{9,25},{17,1},{25,9},{2,18},{10... | collective-permute-start | bytes 1179656 | tf_op jit(solution)/shard_map/ppermute | solution.py:760
  139.7 25.0 %collective-permute-start.21 = (bf16[2,4,96,512]{3,2,1,0:T(8,128)(2,1)S(1)}, bf16[2,4,96,512]{3,2,1,0:T(8,128)(2,1)}, u32[]{:S(2)}, u32[]{:S(2)}) collective-permute-start(bf16[2,4,96,512]{3,2,1,0:T(8,128)(2,1)S(1)} %get-tuple-element.196.refs_11_), channel_id=1, source_target_pairs={{0,16},{8,24},{16,0},{24,8},{1,17},{9,25},{17,1},{25,9},{2,18},{10... | collective-permute-start | bytes 2359304 | tf_op jit(solution)/shard_map/ppermute | solution.py:760
  141.1 27.1 %collective-permute-start.14 = (bf16[2,4,96,512]{3,2,1,0:T(8,128)(2,1)S(1)}, bf16[2,4,96,512]{3,2,1,0:T(8,128)(2,1)}, u32[]{:S(2)}, u32[]{:S(2)}) collective-permute-start(bf16[2,4,96,512]{3,2,1,0:T(8,128)(2,1)S(1)} %get-tuple-element.197.refs_10_), channel_id=1, source_target_pairs={{0,8},{8,0},{16,24},{24,16},{1,9},{9,1},{17,25},{25,17},{2,10},{10... | collective-permute-start | bytes 2359304 | tf_op jit(solution)/shard_map/ppermute | solution.py:760
  154.6 16.2 %collective-permute-start.18 = (bf16[192,512]{1,0:T(8,128)(2,1)S(1)}, bf16[192,512]{1,0:T(8,128)(2,1)S(1)}, u32[]{:S(2)}, u32[]{:S(2)}) collective-permute-start(bf16[192,512]{1,0:T(8,128)(2,1)S(1)} %pad_maximum_fusion.6), channel_id=1, source_target_pairs={{0,2},{1,3},{2,0},{3,1},{4,6},{5,7},{6,4},{7,5},{8,10},{9,11},{10,... | collective-permute-start | bytes 589832 | tf_op jit(solution)/shard_map/ppermute | solution.py:760
  156.1 14.6 %collective-permute-start.19 = (bf16[192,512]{1,0:T(8,128)(2,1)S(1)}, bf16[192,512]{1,0:T(8,128)(2,1)S(1)}, u32[]{:S(2)}, u32[]{:S(2)}) collective-permute-start(bf16[192,512]{1,0:T(8,128)(2,1)S(1)} %pad_maximum_fusion.7), channel_id=1, source_target_pairs={{0,4},{1,5},{2,6},{3,7},{4,0},{5,1},{6,2},{7,3},{8,12},{9,13},{10,... | collective-permute-start | bytes 589832 | tf_op jit(solution)/shard_map/ppermute | solution.py:760
  156.7 17.6 %collective-permute-start.20 = (bf16[192,512]{1,0:T(8,128)(2,1)S(1)}, bf16[192,512]{1,0:T(8,128)(2,1)}, u32[]{:S(2)}, u32[]{:S(2)}) collective-permute-start(bf16[192,512]{1,0:T(8,128)(2,1)S(1)} %pad_maximum_fusion.8), channel_id=1, source_target_pairs={{0,6},{1,7},{2,4},{3,5},{4,2},{5,3},{6,0},{7,1},{8,14},{9,15},{10,... | collective-permute-start | bytes 589832 | tf_op jit(solution)/shard_map/ppermute | solution.py:760
  166.8 10.4 %collective-permute-start.22 = (bf16[4,96,512]{2,1,0:T(8,128)(2,1)}, bf16[4,96,512]{2,1,0:T(8,128)(2,1)}, u32[]{:S(2)}, u32[]{:S(2)}) collective-permute-start(bf16[4,96,512]{2,1,0:T(8,128)(2,1)} %fusion.3), channel_id=1, source_target_pairs={{0,8},{8,0},{16,24},{24,16},{1,9},{9,1},{17,25},{25,17},{2,10},{10... | collective-permute-start | bytes 1179656 | tf_op jit(solution)/shard_map/ppermute | solution.py:760
  170.2 10.0 %collective-permute-start.15 = (bf16[4,96,512]{2,1,0:T(8,128)(2,1)}, bf16[4,96,512]{2,1,0:T(8,128)(2,1)}, u32[]{:S(2)}, u32[]{:S(2)}) collective-permute-start(bf16[4,96,512]{2,1,0:T(8,128)(2,1)} %fusion.1), channel_id=1, source_target_pairs={{0,16},{8,24},{16,0},{24,8},{1,17},{9,25},{17,1},{25,9},{2,18},{10... | collective-permute-start | bytes 1179656 | tf_op jit(solution)/shard_map/ppermute | solution.py:760
  182.1 8.0 %collective-permute-start.23 = (bf16[192,512]{1,0:T(8,128)(2,1)S(1)}, bf16[192,512]{1,0:T(8,128)(2,1)S(1)}, u32[]{:S(2)}, u32[]{:S(2)}) collective-permute-start(bf16[192,512]{1,0:T(8,128)(2,1)S(1)} %pad_maximum_fusion.9), channel_id=1, source_target_pairs={{0,2},{1,3},{2,0},{3,1},{4,6},{5,7},{6,4},{7,5},{8,10},{9,11},{10,... | collective-permute-start | bytes 589832 | tf_op jit(solution)/shard_map/ppermute | solution.py:760
  183.6 13.0 %collective-permute-start.24 = (bf16[192,512]{1,0:T(8,128)(2,1)S(1)}, bf16[192,512]{1,0:T(8,128)(2,1)S(1)}, u32[]{:S(2)}, u32[]{:S(2)}) collective-permute-start(bf16[192,512]{1,0:T(8,128)(2,1)S(1)} %pad_maximum_fusion.10), channel_id=1, source_target_pairs={{0,4},{1,5},{2,6},{3,7},{4,0},{5,1},{6,2},{7,3},{8,12},{9,13},{10,... | collective-permute-start | bytes 589832 | tf_op jit(solution)/shard_map/ppermute | solution.py:760
  184.3 16.3 %collective-permute-start.25 = (bf16[192,512]{1,0:T(8,128)(2,1)S(1)}, bf16[192,512]{1,0:T(8,128)(2,1)S(1)}, u32[]{:S(2)}, u32[]{:S(2)}) collective-permute-start(bf16[192,512]{1,0:T(8,128)(2,1)S(1)} %pad_maximum_fusion.11), channel_id=1, source_target_pairs={{0,6},{1,7},{2,4},{3,5},{4,2},{5,3},{6,0},{7,1},{8,14},{9,15},{10,... | collective-permute-start | bytes 589832 | tf_op jit(solution)/shard_map/ppermute | solution.py:760
  186.8 16.4 %collective-permute-start.31 = (bf16[192,512]{1,0:T(8,128)(2,1)S(1)}, bf16[192,512]{1,0:T(8,128)(2,1)S(1)}, u32[]{:S(2)}, u32[]{:S(2)}) collective-permute-start(bf16[192,512]{1,0:T(8,128)(2,1)S(1)} %add_convert_fusion.8.p0), channel_id=1, source_target_pairs={{0,24},{8,16},{16,8},{24,0},{1,25},{9,17},{17,9},{25,1},{2,26},{10... | collective-permute-start | bytes 589832 | tf_op jit(solution)/shard_map/ppermute | solution.py:760
  187.6 16.6 %collective-permute-start.30 = (bf16[192,512]{1,0:T(8,128)(2,1)S(1)}, bf16[192,512]{1,0:T(8,128)(2,1)S(1)}, u32[]{:S(2)}, u32[]{:S(2)}) collective-permute-start(bf16[192,512]{1,0:T(8,128)(2,1)S(1)} %add_convert_fusion.8.p0), channel_id=1, source_target_pairs={{0,16},{8,24},{16,0},{24,8},{1,17},{9,25},{17,1},{25,9},{2,18},{10... | collective-permute-start | bytes 589832 | tf_op jit(solution)/shard_map/ppermute | solution.py:760
  190.1 14.2 %collective-permute-start.29 = (bf16[192,512]{1,0:T(8,128)(2,1)S(1)}, bf16[192,512]{1,0:T(8,128)(2,1)S(1)}, u32[]{:S(2)}, u32[]{:S(2)}) collective-permute-start(bf16[192,512]{1,0:T(8,128)(2,1)S(1)} %add_convert_fusion.8.p0), channel_id=1, source_target_pairs={{0,8},{8,0},{16,24},{24,16},{1,9},{9,1},{17,25},{25,17},{2,10},{10... | collective-permute-start | bytes 589832 | tf_op jit(solution)/shard_map/ppermute | solution.py:760
  200.7 8.4 %collective-permute-start.28 = (bf16[192,512]{1,0:T(8,128)(2,1)S(1)}, bf16[192,512]{1,0:T(8,128)(2,1)S(1)}, u32[]{:S(2)}, u32[]{:S(2)}) collective-permute-start(bf16[192,512]{1,0:T(8,128)(2,1)S(1)} %add_convert_fusion.9.p0), channel_id=1, source_target_pairs={{0,24},{8,16},{16,8},{24,0},{1,25},{9,17},{17,9},{25,1},{2,26},{10... | collective-permute-start | bytes 589832 | tf_op jit(solution)/shard_map/ppermute | solution.py:760
  201.7 9.1 %collective-permute-start.27 = (bf16[192,512]{1,0:T(8,128)(2,1)S(1)}, bf16[192,512]{1,0:T(8,128)(2,1)S(1)}, u32[]{:S(2)}, u32[]{:S(2)}) collective-permute-start(bf16[192,512]{1,0:T(8,128)(2,1)S(1)} %add_convert_fusion.9.p0), channel_id=1, source_target_pairs={{0,16},{8,24},{16,0},{24,8},{1,17},{9,25},{17,1},{25,9},{2,18},{10... | collective-permute-start | bytes 589832 | tf_op jit(solution)/shard_map/ppermute | solution.py:760
  203.2 7.6 %collective-permute-start.26 = (bf16[192,512]{1,0:T(8,128)(2,1)S(1)}, bf16[192,512]{1,0:T(8,128)(2,1)S(1)}, u32[]{:S(2)}, u32[]{:S(2)}) collective-permute-start(bf16[192,512]{1,0:T(8,128)(2,1)S(1)} %add_convert_fusion.9.p0), channel_id=1, source_target_pairs={{0,8},{8,0},{16,24},{24,16},{1,9},{9,1},{17,25},{25,17},{2,10},{10... | collective-permute-start | bytes 589832 | tf_op jit(solution)/shard_map/ppermute | solution.py:760
  (33 other events, 239.1 us)
